TPU v7x, 1024 devices: a whole 8x8x8 slice. The times are simulated.
1024 devices in a mesh: grp: 16 (over x, core), rep: 64 (over z, y).
Axes of the slice: x: 8, y: 8, z: 8, core: 2. Of those that a mesh axis runs over, the one named last changes fastest.
Arguments:
- features: bfloat16 [524288, 768], P(('grp', 'rep')), may hold values from -6 to 6
- fetch_row: int32 [256, 4096], P('grp', 'rep'), may hold values from 0 to 511
- live_count: int32 [256, 64], P('grp', 'rep'), may hold values from 16 to 64, as said below
- seed_features: bfloat16 [524288, 768], P(('grp', 'rep')), may hold values from -6 to 6
- tile_block: int32 [4096, 8], P(('grp', 'rep')), may hold values from 0 to 7, each once within a row
- tile_weight: bfloat16 [4096, 8, 128, 128], P(('grp', 'rep')), may hold values from -0.1875 to 0.1875
- self_weight: bfloat16 [768, 512], replicated, may hold values from -0.21875 to 0.21875
- neighbour_weight: bfloat16 [768, 512], replicated, may hold values from -0.21875 to 0.21875
- layer_bias: float32 [512], replicated, may hold values from -4 to 4
- cotangent: bfloat16 [524288, 512], P(('grp', 'rep')), may hold values from -24 to 24
Outputs:
- weight_grad: float32 [512, 768], P('grp', 'rep')
Inputs may be any that keep to these rules, and one draw needn't show every extreme that they name: `live_count`: slots at or past the count are padding. In every draw, for each rep index some owner is asked for all 64 slots by every device of its group. `tile_block`: each row names every block of a device's fetched rows once.
All inputs are finite; a program needn't handle non-finite values.
Results may differ from a plain program's by a relative error of at most 0.0043.
Values may be sent and summed in bfloat16 or wider, within the bound.
No kernel may reach another device: no remote copies, remote signals or barrier semaphores. Data moves between devices by JAX's collectives and lax.ppermute only.
A program may use at most 32 MiB of HBM per device.

v0:
```python
import jax
import jax.numpy as jnp
from jax import lax
from jax.sharding import PartitionSpec as P


def body(
    features,
    fetch_row,
    live_count,
    seed_features,
    tile_block,
    tile_weight,
    self_weight,
    neighbour_weight,
    layer_bias,
    cotangent,
):
    width = features.shape[1]
    asked = lax.all_to_all(fetch_row, "grp", split_axis=0, concat_axis=0, tiled=True)
    table_rows = jnp.take(features, asked.reshape(-1), axis=0).reshape(asked.shape + (width,))
    fetched = lax.all_to_all(table_rows, "grp", split_axis=0, concat_axis=0, tiled=True)
    live_mask = lax.broadcasted_iota(jnp.int32, fetch_row.shape, 1) < live_count
    fetched = jnp.where(live_mask[:, :, None], fetched, jnp.zeros((), fetched.dtype))
    row_blocks = fetched.reshape(-1, 128, width)
    chosen = jnp.take(row_blocks, tile_block, axis=0)
    aggregated = jnp.einsum(
        "bkij,bkjf->bif", tile_weight, chosen, preferred_element_type=jnp.float32
    )
    aggregated = aggregated.reshape(-1, width).astype(jnp.bfloat16)
    pre_act = jnp.dot(seed_features, self_weight, preferred_element_type=jnp.float32)
    pre_act = pre_act + jnp.dot(aggregated, neighbour_weight, preferred_element_type=jnp.float32)
    pre_act = pre_act + layer_bias[None, :]
    sigmoid_val = jax.nn.sigmoid(pre_act)
    slope = sigmoid_val * (1.0 + pre_act * (1.0 - sigmoid_val))
    grad_pre = (cotangent.astype(jnp.float32) * slope).astype(jnp.bfloat16)
    partial_sum = lax.psum_scatter(
        lax.dot_general(
            grad_pre, aggregated, (((0,), (0,)), ((), ())), preferred_element_type=jnp.float32
        ),
        "grp",
        scatter_dimension=0,
        tiled=True,
    )
    return lax.psum_scatter(partial_sum, "rep", scatter_dimension=1, tiled=True)


def solution(mesh):
    placed = (
        P(("grp", "rep"), None),
        P("grp", "rep"),
        P("grp", "rep"),
        P(("grp", "rep"), None),
        P(("grp", "rep"), None),
        P(("grp", "rep"), None, None, None),
        P(),
        P(),
        P(),
        P(("grp", "rep"), None),
    )
    return jax.shard_map(
        body, mesh=mesh, in_specs=placed, out_specs=P("grp", "rep"), check_vma=False
    )
```

profile of v0, /device:TPU:2, one launch (start us, length us, event | category | flops | bytes accessed | tf_op | source)
XLA Modules:
  0.0 334.8 jit_solution(8291727832867941134)
XLA Ops:
  6.5 0.0 copy-start
  6.5 22.7 %all_to_all.14 = s32[16,1,64]{2,1,0:T(1,128)S(1)} all-to-all(s32[16,1,64]{2,1,0:T(1,128)} %bitcast.27), channel_id=1, replica_groups=mesh['grp'=16,'rep'=64] {'grp'}, dimensions={0} | all-to-all | bytes 8192 | tf_op jit(solution)/shard_map/all_to_all | solution.py:20
  29.3 0.5 broadcast.66
  29.8 0.7 reduce.3
  30.5 0.1 reshape.82
  30.6 5.7 %gather_fusion = bf16[1024,768]{1,0:T(8,128)(2,1)S(1)} fusion(bf16[512,768]{1,0:T(8,128)(2,1)} %param.10, s32[1024]{0:T(1024)S(1)} %broadcast_clamp_fusion), kind=kCustom, calls=%fused_computation | custom fusion | bytes 3149824 | tf_op jit(solution)/shard_map/jit(_take)/gather | solution.py:21
  36.3 1.4 broadcast_select_fusion
  37.7 0.0 copy-start.4
  37.7 0.0 copy-start.5
  37.7 0.0 copy-start.2
  37.7 0.0 copy-start.3
  37.7 5.8 %all-to-all-start.1 = ((bf16[16,64,768]{2,1,0:T(8,128)(2,1)}), bf16[16,64,768]{2,1,0:T(8,128)(2,1)}, u32[]{:S(2)}, u32[]{:S(2)}) async-start(bf16[16,64,768]{2,1,0:T(8,128)(2,1)} %broadcast_select_fusion), calls=%async_computation.1 | async-start | bytes 3145728 | tf_op jit(solution)/shard_map/all_to_all | solution.py:22
  43.4 0.0 reduce-scatter.3.cloned.1.call-start
  43.5 0.0 copy-done.4
  43.5 0.1 reshape.94
  43.6 0.0 copy-done.5
  43.6 0.1 iota_compare_fusion
  43.7 0.0 copy-done.2
  43.7 0.0 copy-done.3
  43.7 1.6 fusion.13
  45.3 34.3 %all-to-all-done.1 = bf16[16,64,768]{2,1,0:T(8,128)(2,1)} async-done(((bf16[16,64,768]{2,1,0:T(8,128)(2,1)}), bf16[16,64,768]{2,1,0:T(8,128)(2,1)}, u32[]{:S(2)}, u32[]{:S(2)}) %all-to-all-start.1) | async-done | bytes 1572896 | tf_op jit(solution)/shard_map/all_to_all | solution.py:22
  79.6 1.6 broadcast_select_fusion.1
  81.2 3.6 %gather_fusion.1 = bf16[32,128,768]{2,1,0:T(8,128)(2,1)} fusion(bf16[8,128,768]{2,1,0:T(8,128)(2,1)S(1)} %bitcast.22, s32[1024]{0:T(1024)S(1)} %pad_clamp_fusion), kind=kCustom, calls=%fused_computation.1 | custom fusion | bytes 12583040 | tf_op jit(solution)/shard_map/jit(_take)/gather | solution.py:26
  84.8 0.0 copy-done
  84.8 0.0 copy-start.1
  84.8 0.0 copy-start.6
  84.8 0.0 copy-start.7
  84.9 0.0 copy-start.8
  84.9 5.2 %bitcast_convert_fusion = bf16[4,768,128]{1,2,0:T(8,128)(2,1)} fusion(bf16[4,8,128,128]{3,2,1,0:T(8,128)(2,1)S(1)} %copy-done, bf16[4,8,128,768]{3,2,1,0:T(8,128)(2,1)} %bitcast.23, pred[4,8]{1,0:T(4,128)(4,1)S(1)} %compare_and_fusion.1), kind=kOutput, calls=%fused_computation.6 | convolution fusion | flops 808845312 | bytes 8126496 | tf_op jit(solution)/shard_map/bkij,bkjf->bif/dot_general | solution.py:27
  90.1 0.0 copy-done.1
  90.1 0.0 copy-done.6
  90.1 0.0 copy-done.7
  90.1 0.0 copy-done.8
  90.1 3.9 %fusion.7 = f32[512,768]{1,0:T(8,128)} fusion(bf16[512,768]{1,0:T(8,128)(2,1)} %bitcast.29, f32[512,512]{1,0:T(8,128)S(1)} %copy-done.1, bf16[768,512]{1,0:T(8,128)(2,1)S(1)} %copy-done.6, bf16[512,512]{1,0:T(8,128)(2,1)S(1)} %copy-done.7, f32[512]{0:T(512)S(1)} %copy-done.8), kind=kOutput, calls=%fused_computation.12 | convolution fusion | flops 808452096 | bytes 4720640 | tf_op jit(solution)/shard_map/dot_general | solution.py:38
  94.0 0.0 reduce-scatter.3.cloned.1.call-update
  94.0 0.0 all-reduce.3.cloned.1.call-start
  94.1 61.6 %reduce-scatter.3.cloned.1.call-done = f32[32,768]{1,0:T(8,128)} async-done(((f32[512,768]{1,0:T(8,128)}), f32[32,768]{1,0:T(8,128)}) %reduce-scatter.3.cloned.1.call-update) | async-done | bytes 98320 | tf_op jit(solution)/shard_map/reduce_scatter | solution.py:37
  155.7 0.0 all-reduce.3.cloned.1.call-update
  155.7 1.3 dynamic-slice
  157.6 168.8 %all-reduce.3.cloned.1.call-done = f32[32,768]{1,0:T(8,128)} async-done(((f32[32,768]{1,0:T(8,128)}), f32[32,768]{1,0:T(8,128)}) %all-reduce.3.cloned.1.call-update) | async-done | bytes 98320
  326.4 0.8 constant_dynamic-slice_fusion
  327.2 0.7 copy.12
  (6 shorter events, 0.0 us)
Async XLA Ops:
  6.5 78.3 %copy-start = (bf16[4,8,128,128]{3,2,1,0:T(8,128)(2,1)S(1)}, bf16[4,8,128,128]{3,2,1,0:T(8,128)(2,1)}, u32[]{:S(2)}) copy-start(bf16[4,8,128,128]{3,2,1,0:T(8,128)(2,1)} %param.15) | copy-start | bytes 3145732
  37.7 5.8 %copy-start.4 = (s32[4,8]{1,0:T(4,128)S(1)}, s32[4,8]{1,0:T(4,128)}, u32[]{:S(2)}) copy-start(s32[4,8]{1,0:T(4,128)} %param.14) | copy-start | bytes 388
  37.7 5.9 %copy-start.5 = (s32[16,1]{0,1:T(1,128)S(1)}, s32[16,1]{0,1:T(1,128)}, u32[]{:S(2)}) copy-start(s32[16,1]{0,1:T(1,128)} %param.12) | copy-start | bytes 196
  37.7 6.0 %copy-start.2 = (bf16[512,768]{1,0:T(8,128)(2,1)S(1)}, bf16[512,768]{1,0:T(8,128)(2,1)}, u32[]{:S(2)}) copy-start(bf16[512,768]{1,0:T(8,128)(2,1)} %param.13) | copy-start | bytes 2359300
  37.7 6.0 %copy-start.3 = (bf16[768,512]{1,0:T(8,128)(2,1)S(1)}, bf16[768,512]{1,0:T(8,128)(2,1)}, u32[]{:S(2)}) copy-start(bf16[768,512]{1,0:T(8,128)(2,1)} %param.16) | copy-start | bytes 2359300
  37.7 41.9 %all-to-all-start.1 = ((bf16[16,64,768]{2,1,0:T(8,128)(2,1)}), bf16[16,64,768]{2,1,0:T(8,128)(2,1)}, u32[]{:S(2)}, u32[]{:S(2)}) async-start(bf16[16,64,768]{2,1,0:T(8,128)(2,1)} %broadcast_select_fusion), calls=%async_computation.1 | async-start | bytes 3145728 | tf_op jit(solution)/shard_map/all_to_all | solution.py:22
  43.4 112.2 %reduce-scatter.3.cloned.1.call-start = ((), (), s32[]{:S(2)}) async-start(), calls=%async_computation.3 | async-start | bytes 1671168 | tf_op jit(solution)/shard_map/reduce_scatter | solution.py:37
  84.8 5.3 %copy-start.1 = (f32[512,512]{1,0:T(8,128)S(1)}, f32[512,512]{1,0:T(8,128)}, u32[]{:S(2)}) copy-start(f32[512,512]{1,0:T(8,128)} %fusion.13) | copy-start | bytes 3145732
  84.8 5.3 %copy-start.6 = (bf16[768,512]{1,0:T(8,128)(2,1)S(1)}, bf16[768,512]{1,0:T(8,128)(2,1)}, u32[]{:S(2)}) copy-start(bf16[768,512]{1,0:T(8,128)(2,1)} %param.17) | copy-start | bytes 2359300
  84.8 5.3 %copy-start.7 = (bf16[512,512]{1,0:T(8,128)(2,1)S(1)}, bf16[512,512]{1,0:T(8,128)(2,1)}, u32[]{:S(2)}) copy-start(bf16[512,512]{1,0:T(8,128)(2,1)} %param.19) | copy-start | bytes 1572868
  84.9 5.3 %copy-start.8 = (f32[512]{0:T(512)S(1)}, f32[512]{0:T(512)}, u32[]{:S(2)}) copy-start(f32[512]{0:T(512)} %param.18) | copy-start | bytes 6148
  94.0 232.4 %all-reduce.3.cloned.1.call-start = ((), (), s32[]{:S(2)}) async-start(), calls=%async_computation.4 | async-start | bytes 196608
Sparse Core Ops, SparseCore 0:
  94.1 61.4 reduce-scatter.2
  159.3 167.1 all-reduce.2
where the time goes:
time: 335 us
  waiting for transfers between devices  265 us (79%)
  blocking collectives  22.7 us (7%)
  between operations  14.2 us (4%)
  local copies, waits for them, and re-layouts  12.8 us (4%)
  matrix products  10.7 us (3%)
  starting transfers between devices  5.83 us (2%)
  other arithmetic  3.77 us (1%)
    unnamed x3, waiting for transfers between devices  169 us
    reduce_scatter x1, waiting for transfers between devices, body(): lax.psum_scatter(lax.dot_general(grad_pre, aggregated, (((0,), (0,)), (()...  61.6 us
    all_to_all x1, waiting for transfers between devices, body(): lax.all_to_all(table_rows, 'grp', split_axis=0, concat_axis=0, tiled=True)  34.3 us
    all_to_all x1, blocking collectives, body(): lax.all_to_all(fetch_row, 'grp', split_axis=0, concat_axis=0, tiled=True)  22.7 us
  transfers between devices with their start and end apart: 3, of which 3 were waited for; matrix products, arithmetic and copies ran while one was open for 1% of the time, Pallas kernels for 0%

commit v1 on v0

v1 whole, which is shorter than its diff:
```python
import functools

import jax
import jax.numpy as jnp
from jax import lax
from jax.experimental import pallas as pl
from jax.experimental.pallas import tpu as pltpu
from jax.sharding import Mesh, PartitionSpec as P

F32 = jnp.float32
BF16 = jnp.bfloat16
GRP = ("x", "c")
REP = ("z", "y")
EVERY = GRP + REP
VMEM_LIMIT = 24 * 1024 * 1024


def whole(shape):
    return pl.BlockSpec(shape, lambda *_: (0,) * len(shape))


def params(grid_dims=0):
    semantics = ("arbitrary",) * grid_dims if grid_dims else None
    return pltpu.CompilerParams(vmem_limit_bytes=VMEM_LIMIT, dimension_semantics=semantics)


def pick_kernel(asked_ref, table_ref, out_ref, hot_ref):
    owners, slots = asked_ref.shape[0], asked_ref.shape[2]
    rows = table_ref.shape[0]
    line = lax.broadcasted_iota(jnp.int32, (slots, slots), 0)
    lane = lax.broadcasted_iota(jnp.int32, (slots, slots), 1)
    row_ix = lax.broadcasted_iota(jnp.int32, (slots, rows), 1).astype(F32)
    for p in range(owners):
        asked = jnp.broadcast_to(asked_ref[p].astype(F32), (slots, slots))
        column = jnp.sum(jnp.where(line == lane, asked, 0.0), axis=1, keepdims=True)
        hot_ref[p * slots : (p + 1) * slots, :] = jnp.where(row_ix == column, 1.0, 0.0).astype(BF16)
    out_ref[...] = jnp.dot(hot_ref[...], table_ref[...], preferred_element_type=F32).astype(BF16)


def pick_rows(asked, table):
    owners, _, slots = asked.shape
    rows, width = table.shape
    step = owners // 4
    return pl.pallas_call(
        pick_kernel,
        grid=(4,),
        out_shape=jax.ShapeDtypeStruct((owners * slots, width), BF16),
        in_specs=[pl.BlockSpec((step, 1, slots), lambda i: (i, 0, 0)), whole((rows, width))],
        out_specs=pl.BlockSpec((step * slots, width), lambda i: (i, 0)),
        scratch_shapes=[pltpu.VMEM((step * slots, rows), BF16)],
        compiler_params=params(1),
        cost_estimate=pl.CostEstimate(
            flops=2 * owners * slots * rows * width, bytes_accessed=5 * 10**6, transcendentals=0
        ),
        name="pick_rows",
    )(asked, table)


def prepare_kernel(block_ref, live_ref, weight_ref, seed_ref, self_ref, bias_ref, _, adj_ref, own_ref):
    seed_blocks, tiles, side, _ = weight_ref.shape
    slots = adj_ref.shape[1] // live_ref.shape[0]
    lane = lax.broadcasted_iota(jnp.int32, (side, side), 1)
    for b in range(seed_blocks):
        for k in range(tiles):
            block = block_ref[b, k]
            limit = jnp.where(lane < slots, live_ref[2 * block, 0], live_ref[2 * block + 1, 0] + slots)
            tile = jnp.where(lane < limit, weight_ref[b, k].astype(F32), 0.0)
            start = pl.multiple_of(block * side, side)
            adj_ref[b * side : (b + 1) * side, pl.ds(start, side)] = tile.astype(BF16)
    own_ref[...] = (
        jnp.dot(seed_ref[...], self_ref[...], preferred_element_type=F32) + bias_ref[...]
    )


def prepare(tile_block, live_count, tile_weight, seeds, self_weight, bias, after):
    seed_blocks, tiles, side, _ = tile_weight.shape
    targets, width = seeds.shape
    hidden = self_weight.shape[1]
    return pl.pallas_call(
        prepare_kernel,
        out_shape=(
            jax.ShapeDtypeStruct((seed_blocks * side, tiles * side), BF16),
            jax.ShapeDtypeStruct((targets, hidden), F32),
        ),
        in_specs=[
            pl.BlockSpec(memory_space=pltpu.SMEM),
            pl.BlockSpec(memory_space=pltpu.SMEM),
            pl.BlockSpec(memory_space=pltpu.VMEM),
            pl.BlockSpec(memory_space=pltpu.VMEM),
            pl.BlockSpec(memory_space=pltpu.VMEM),
            pl.BlockSpec(memory_space=pltpu.VMEM),
            pl.BlockSpec(memory_space=pl.ANY),
        ],
        out_specs=(pl.BlockSpec(memory_space=pltpu.VMEM), pl.BlockSpec(memory_space=pltpu.VMEM)),
        compiler_params=params(),
        cost_estimate=pl.CostEstimate(
            flops=2 * targets * width * hidden, bytes_accessed=6 * 10**6, transcendentals=0
        ),
        name="prepare",
    )(tile_block, live_count, tile_weight, seeds, self_weight, bias.reshape(1, -1), after)


def layer_kernel(core_ref, adj_ref, rows_ref, neigh_ref, own_ref, cot_ref, keep_ref, send_ref, agg_ref, pre_ref, grad_ref, out_ref):
    step, last = pl.program_id(0), pl.num_programs(0) - 1
    chunk = rows_ref.shape[1]
    agg = jnp.dot(adj_ref[...], rows_ref[...], preferred_element_type=F32).astype(BF16)
    agg_ref[:, pl.ds(pl.multiple_of(step * chunk, chunk), chunk)] = agg
    part = jnp.dot(agg, neigh_ref[...], preferred_element_type=F32)

    @pl.when(step == 0)
    def _():
        pre_ref[...] = own_ref[...] + part

    @pl.when((step > 0) & (step < last))
    def _():
        pre_ref[...] = pre_ref[...] + part

    @pl.when(step == last)
    def _():
        pre = pre_ref[...] + part
        s = 1.0 / (1.0 + jnp.exp(-pre))
        slope = s * (1.0 + pre * (1.0 - s))
        grad_ref[...] = (cot_ref[...].astype(F32) * slope).astype(BF16)
        out_ref[...] = lax.dot_general(
            grad_ref[...], agg_ref[...], (((0,), (0,)), ((), ())), preferred_element_type=F32
        )
        core = core_ref[0]
        groups, span = keep_ref.shape[0], keep_ref.shape[1]
        for x in range(groups):
            mine = pl.multiple_of((2 * x + core) * span, span)
            other = pl.multiple_of((2 * x + 1 - core) * span, span)
            keep_ref[x] = out_ref[pl.ds(mine, span), :]
            send_ref[x] = out_ref[pl.ds(other, span), :].astype(BF16)


def layer(core, adj, rows, neigh, own, cot, span):
    targets, fetched = adj.shape
    width, hidden = neigh.shape
    chunk = 256
    shape = (hidden // (2 * span), span, width)
    return pl.pallas_call(
        layer_kernel,
        grid=(width // chunk,),
        out_shape=(jax.ShapeDtypeStruct(shape, F32), jax.ShapeDtypeStruct(shape, BF16)),
        in_specs=[
            pl.BlockSpec(memory_space=pltpu.SMEM),
            whole((targets, fetched)),
            pl.BlockSpec((fetched, chunk), lambda i: (0, i)),
            pl.BlockSpec((chunk, hidden), lambda i: (i, 0)),
            whole((targets, hidden)),
            whole((targets, hidden)),
        ],
        out_specs=(whole(shape), whole(shape)),
        scratch_shapes=[
            pltpu.VMEM((targets, width), BF16),
            pltpu.VMEM((targets, hidden), F32),
            pltpu.VMEM((targets, hidden), BF16),
            pltpu.VMEM((hidden, width), F32),
        ],
        compiler_params=params(1),
        cost_estimate=pl.CostEstimate(
            flops=2 * targets * width * (fetched + 2 * hidden),
            bytes_accessed=8 * 10**6,
            transcendentals=targets * hidden,
        ),
        name="layer",
    )(core, adj, rows, neigh, own, cot)


def body(
    features,
    fetch_row,
    live_count,
    seed_features,
    tile_block,
    tile_weight,
    self_weight,
    neighbour_weight,
    layer_bias,
    cotangent,
):
    owners, slots = fetch_row.shape
    width, hidden = neighbour_weight.shape
    nx, nc, nz, ny = (lax.axis_size(a) for a in EVERY)
    span = hidden // (nx * nc)
    asked = lax.all_to_all(fetch_row.reshape(owners, 1, slots), GRP, split_axis=0, concat_axis=0, tiled=True)
    picked = pick_rows(asked, features)
    rows = lax.all_to_all(picked.reshape(owners, slots, width), GRP, split_axis=0, concat_axis=0, tiled=True)
    adj, own = prepare(tile_block, live_count, tile_weight, seed_features, self_weight, layer_bias, picked)
    core = lax.axis_index("c").astype(jnp.int32).reshape(1)
    keep, send = layer(core, adj, rows.reshape(owners * slots, width), neighbour_weight, own, cotangent, span)
    got = lax.ppermute(send, "c", [(0, 1), (1, 0)])
    pair = (keep + got.astype(F32)).astype(BF16)
    parts = lax.all_to_all(pair, "x", split_axis=0, concat_axis=0, tiled=True)
    ring = jnp.sum(parts.astype(F32), axis=0)
    cols = width // (nz * ny)
    pieces = ring.reshape(span, nz * ny, cols).transpose(1, 0, 2).reshape(nz * ny, span * cols)
    pieces = lax.all_to_all(pieces, REP, split_axis=0, concat_axis=0, tiled=True)
    return jnp.sum(pieces, axis=0).reshape(span, cols)


def solution(mesh):
    n_grp, n_rep = mesh.shape["grp"], mesh.shape["rep"]
    chips, lines = n_grp // 2, int(round(n_rep**0.5))
    fine = Mesh(mesh.devices.reshape(chips, 2, lines, n_rep // lines), EVERY)
    placed = (
        P(EVERY, None),
        P(GRP, REP),
        P(GRP, REP),
        P(EVERY, None),
        P(EVERY, None),
        P(EVERY, None, None, None),
        P(),
        P(),
        P(),
        P(EVERY, None),
    )
    return jax.shard_map(body, mesh=fine, in_specs=placed, out_specs=P(GRP, REP), check_vma=False)
```

time: 335 us -> 129 us (0.39)
  the two profiles are of different devices: /device:TPU:2 before, /device:TPU:16 now
where the time goes in v1:
time: 129 us; the launch traced here: 128 us
  blocking collectives  68 us (53%)
  waiting for transfers between devices  34.5 us (27%)
  local copies, waits for them, and re-layouts  10.4 us (8%)
  Pallas kernels  8.09 us (6%)
  starting transfers between devices  6.71 us (5%)
    all_to_all x1, blocking collectives, body(): lax.all_to_all(pieces, REP, split_axis=0, concat_axis=0, tiled=True)  34.8 us
    all_to_all x1, waiting for transfers between devices, body(): lax.all_to_all(picked.reshape(owners, slots, width), GRP, split_axis=0, c...  33.2 us
    all_to_all x1, blocking collectives, body(): parts = lax.all_to_all(pair, 'x', split_axis=0, concat_axis=0, tiled=True)  18.9 us
    all_to_all x1, blocking collectives, body(): lax.all_to_all(fetch_row.reshape(owners, 1, slots), GRP, split_axis=0, co...  14.4 us
    unnamed x27, local copies, waits for them, and re-layouts  8.95 us
    pallas_call x1, Pallas kernels, layer(): pl.pallas_call(layer_kernel, grid=(width // chunk,), out_shape=(jax.Shape...  3.89 us
    all_to_all x1, starting transfers between devices, body(): lax.all_to_all(picked.reshape(owners, slots, width), GRP, split_axis=0, c...  3.85 us
    ppermute x1, starting transfers between devices, body(): got = lax.ppermute(send, 'c', [(0, 1), (1, 0)])  2.86 us
  transfers between devices with their start and end apart: 2, of which 2 were waited for; matrix products, arithmetic and copies ran while one was open for 0% of the time, Pallas kernels for 1%

profile of v1, /device:TPU:16, one launch (start us, length us, event | category | flops | bytes accessed | tf_op | source)
XLA Modules:
  0.0 128.1 jit_solution(12468170341007769092)
XLA Ops:
  0.0 14.4 %all_to_all.24.asked_ref = s32[16,1,64]{2,1,0:T(1,128)S(1)} all-to-all(s32[16,1,64]{2,1,0:T(1,128)} %bitcast.13), channel_id=1, replica_groups=mesh['x'=8,'c'=2,'z'=8,'y'=8] {'x','c'}, dimensions={0} | all-to-all | bytes 8192 | tf_op jit(solution)/shard_map/all_to_all | solution.py:186
  14.4 0.0 copy-start.9
  14.4 1.1 copy-done.9
  15.5 2.8 %pick_rows.1._ = bf16[1024,768]{1,0:T(8,128)(2,1)} custom-call(s32[16,1,64]{2,1,0:T(1,128)S(1)} %all_to_all.24.asked_ref, bf16[512,768]{1,0:T(8,128)(2,1)S(1)} %copy-done.9), custom_call_target="tpu_custom_call" | custom-call | flops 805306368 | bytes 5000000 | tf_op jit(solution)/shard_map/pick_rows/pallas_call | solution.py:44
  18.3 0.0 copy-start.12
  18.3 0.0 copy-start
  18.3 0.0 copy-start.1
  18.3 0.0 copy-start.3
  18.3 0.0 copy-start.4
  18.3 3.9 %all-to-all-start.1 = ((bf16[16,64,768]{2,1,0:T(8,128)(2,1)}), bf16[16,64,768]{2,1,0:T(8,128)(2,1)S(1)}, u32[]{:S(2)}, u32[]{:S(2)}) async-start(bf16[16,64,768]{2,1,0:T(8,128)(2,1)} %bitcast.3), calls=%async_computation.1 | async-start | bytes 3145728 | tf_op jit(solution)/shard_map/all_to_all | solution.py:188
  22.2 0.0 copy-done.12
  22.2 0.1 copy.15.live_ref
  22.3 0.0 copy-done
  22.3 0.0 copy-done.1
  22.3 0.0 copy-done.3
  22.3 0.0 copy-done.4
  22.3 0.0 copy-start.2
  22.3 1.1 copy-done.2
  23.4 1.4 %prepare.1 = (bf16[512,1024]{1,0:T(8,128)(2,1)S(1)}, f32[512,512]{1,0:T(8,128)S(1)}) custom-call(s32[4,8]{1,0:T(4,128)S(1)} %copy-done.3, s32[16,1]{1,0:T(8,128)S(1)} %copy.15.live_ref, bf16[4,8,128,128]{3,2,1,0:T(8,128)(2,1)S(1)} %copy-done, bf16[512,768]{1,0:T(8,128)(2,1)S(1)} %copy-done.1, bf16[768,512]{1,0:T(8,128)(2,1)S(1)} %copy-done.2, ...), custom_call_target="tpu_custom_call" | custom-call | flops 402653184 | bytes 6000000 | tf_op jit(solution)/shard_map/prepare/pallas_call | solution.py:79
  24.8 0.0 copy-start.5
  24.9 1.0 copy-done.5
  25.8 0.0 copy-start.7
  25.8 1.0 copy-done.7
  26.8 33.2 %all-to-all-done.1 = bf16[16,64,768]{2,1,0:T(8,128)(2,1)S(1)} async-done(((bf16[16,64,768]{2,1,0:T(8,128)(2,1)}), bf16[16,64,768]{2,1,0:T(8,128)(2,1)S(1)}, u32[]{:S(2)}, u32[]{:S(2)}) %all-to-all-start.1) | async-done | bytes 1572896 | tf_op jit(solution)/shard_map/all_to_all | solution.py:188
  60.0 0.0 copy-start.6
  60.0 1.2 copy-done.6
  61.2 0.0 copy-start.8
  61.2 1.2 copy-done.8
  62.4 0.0 copy-start.10
  62.4 1.1 copy-done.10
  63.6 0.0 copy-start.11
  63.6 1.0 copy-done.11
  64.6 3.9 %layer.1 = (f32[8,32,768]{2,1,0:T(8,128)S(1)}, bf16[8,32,768]{2,1,0:T(8,128)(2,1)S(1)}) custom-call(s32[1]{0:T(128)} %bitcast.core_ref, bf16[512,1024]{1,0:T(8,128)(2,1)S(1)} %copy-done.6, bf16[1024,768]{1,0:T(8,128)(2,1)S(1)} %bitcast.10, bf16[768,512]{1,0:T(8,128)(2,1)S(1)} %copy-done.10, f32[512,512]{1,0:T(8,128)S(1)} %copy-done.8, ...), custom_call_target="tpu_custom_call" | custom-call | flops 1610612736 | bytes 8000000 | tf_op jit(solution)/shard_map/layer/pallas_call | solution.py:141
  68.5 2.9 %collective-permute-start = (bf16[8,32,768]{2,1,0:T(8,128)(2,1)S(1)}, bf16[8,32,768]{2,1,0:T(8,128)(2,1)S(1)}, u32[]{:S(2)}, u32[]{:S(2)}) collective-permute-start(bf16[8,32,768]{2,1,0:T(8,128)(2,1)S(1)} %get-tuple-element.12), channel_id=1, source_target_pairs={{0,64},{64,0},{1,65},{65,1},{2,66},{66,2},{3,67},{67,3},{4,68},{68... | collective-permute-start | bytes 1179656 | tf_op jit(solution)/shard_map/ppermute | solution.py:192
  71.4 1.3 %collective-permute-done = bf16[8,32,768]{2,1,0:T(8,128)(2,1)S(1)} collective-permute-done((bf16[8,32,768]{2,1,0:T(8,128)(2,1)S(1)}, bf16[8,32,768]{2,1,0:T(8,128)(2,1)S(1)}, u32[]{:S(2)}, u32[]{:S(2)}) %collective-permute-start) | collective-permute-done | bytes 393248 | tf_op jit(solution)/shard_map/ppermute | solution.py:192
  72.7 0.1 add_convert_fusion
  72.8 18.9 %all_to_all.25 = bf16[8,32,768]{2,1,0:T(8,128)(2,1)S(1)} all-to-all(bf16[8,32,768]{2,1,0:T(8,128)(2,1)S(1)} %add_convert_fusion), channel_id=1, replica_groups=mesh['x'=8,'c'=2,'z'=8,'y'=8] {'x'}, dimensions={0} | all-to-all | bytes 786432 | tf_op jit(solution)/shard_map/all_to_all | solution.py:194
  91.7 0.1 convert_reduce_fusion
  91.7 0.2 copy.16
  92.0 0.3 copy.17
  92.3 0.1 copy.18
  92.4 34.8 %all_to_all.26 = f32[64,1,384]{2,1,0:T(1,128)S(1)} all-to-all(f32[64,1,384]{2,1,0:T(1,128)S(1)} %copy.18), channel_id=1, replica_groups=mesh['x'=8,'c'=2,'z'=8,'y'=8] {'z','y'}, dimensions={0} | all-to-all | bytes 196608 | tf_op jit(solution)/shard_map/all_to_all | solution.py:198
  127.2 0.1 reduce_sum.19
  127.3 0.1 reshape.31
  127.4 0.7 copy.19
  (2 shorter events, 0.1 us)
Async XLA Ops:
  14.4 1.1 copy-start.9
  18.3 3.9 %copy-start.12 = (s32[16,1]{0,1:T(1,128)S(1)}, s32[16,1]{0,1:T(1,128)}, u32[]{:S(2)}) copy-start(s32[16,1]{0,1:T(1,128)} %param.12) | copy-start | bytes 196
  18.3 4.0 %copy-start = (bf16[4,8,128,128]{3,2,1,0:T(8,128)(2,1)S(1)}, bf16[4,8,128,128]{3,2,1,0:T(8,128)(2,1)}, u32[]{:S(2)}) copy-start(bf16[4,8,128,128]{3,2,1,0:T(8,128)(2,1)} %weight_ref.1) | copy-start | bytes 3145732
  18.3 4.0 %copy-start.1 = (bf16[512,768]{1,0:T(8,128)(2,1)S(1)}, bf16[512,768]{1,0:T(8,128)(2,1)}, u32[]{:S(2)}) copy-start(bf16[512,768]{1,0:T(8,128)(2,1)} %seed_ref.1) | copy-start | bytes 2359300
  18.3 4.0 %copy-start.3 = (s32[4,8]{1,0:T(4,128)S(1)}, s32[4,8]{1,0:T(4,128)}, u32[]{:S(2)}) copy-start(s32[4,8]{1,0:T(4,128)} %block_ref.1) | copy-start | bytes 388
  18.3 4.0 %copy-start.4 = (f32[512]{0:T(512)S(1)}, f32[512]{0:T(512)}, u32[]{:S(2)}) copy-start(f32[512]{0:T(512)} %param.18) | copy-start | bytes 6148
  18.3 41.7 %all-to-all-start.1 = ((bf16[16,64,768]{2,1,0:T(8,128)(2,1)}), bf16[16,64,768]{2,1,0:T(8,128)(2,1)S(1)}, u32[]{:S(2)}, u32[]{:S(2)}) async-start(bf16[16,64,768]{2,1,0:T(8,128)(2,1)} %bitcast.3), calls=%async_computation.1 | async-start | bytes 3145728 | tf_op jit(solution)/shard_map/all_to_all | solution.py:188
  22.3 1.1 copy-start.2
  24.8 1.0 copy-start.5
  25.8 1.0 copy-start.7
  60.0 1.2 copy-start.6
  61.2 1.2 copy-start.8
  62.4 1.1 copy-start.10
  63.6 1.0 copy-start.11
  68.5 4.2 %collective-permute-start = (bf16[8,32,768]{2,1,0:T(8,128)(2,1)S(1)}, bf16[8,32,768]{2,1,0:T(8,128)(2,1)S(1)}, u32[]{:S(2)}, u32[]{:S(2)}) collective-permute-start(bf16[8,32,768]{2,1,0:T(8,128)(2,1)S(1)} %get-tuple-element.12), channel_id=1, source_target_pairs={{0,64},{64,0},{1,65},{65,1},{2,66},{66,2},{3,67},{67,3},{4,68},{68... | collective-permute-start | bytes 1179656 | tf_op jit(solution)/shard_map/ppermute | solution.py:192

commit v2 on v1

v2 whole, which is shorter than its diff:
```python
import jax
import jax.numpy as jnp
from jax import lax
from jax.experimental import pallas as pl
from jax.experimental.pallas import tpu as pltpu
from jax.sharding import Mesh, PartitionSpec as P

F32 = jnp.float32
BF16 = jnp.bfloat16
GRP = ("x", "c")
REP = ("z", "y")
EVERY = GRP + REP
VMEM_LIMIT = 24 * 1024 * 1024


def in_hbm(array):
    return pltpu.with_memory_space_constraint(array, pltpu.HBM)


def params():
    return pltpu.CompilerParams(vmem_limit_bytes=VMEM_LIMIT)


def pick_kernel(asked_ref, table_ref, out_ref, table_buf, hot_ref, out_buf, table_sem, out_sems):
    owners, slots = asked_ref.shape[0], asked_ref.shape[2]
    rows = table_ref.shape[0]
    load = pltpu.make_async_copy(table_ref, table_buf, table_sem)
    load.start()
    line = lax.broadcasted_iota(jnp.int32, (slots, slots), 0)
    lane = lax.broadcasted_iota(jnp.int32, (slots, slots), 1)
    row_ix = lax.broadcasted_iota(jnp.int32, (slots, rows), 1).astype(F32)
    for p in range(owners):
        asked = jnp.broadcast_to(asked_ref[p].astype(F32), (slots, slots))
        column = jnp.sum(jnp.where(line == lane, asked, 0.0), axis=1, keepdims=True)
        hot_ref[p * slots : (p + 1) * slots, :] = jnp.where(row_ix == column, 1.0, 0.0).astype(BF16)
    load.wait()
    pieces = out_sems.shape[0]
    size = owners * slots // pieces
    stores = []
    for i in range(pieces):
        part = pl.ds(i * size, size)
        out_buf[part, :] = jnp.dot(hot_ref[part, :], table_buf[...], preferred_element_type=F32).astype(BF16)
        stores.append(pltpu.make_async_copy(out_buf.at[part], out_ref.at[part], out_sems.at[i]))
        stores[i].start()
    for store in stores:
        store.wait()


def pick_rows(asked, table):
    owners, _, slots = asked.shape
    rows, width = table.shape
    pieces = 4
    return pl.pallas_call(
        pick_kernel,
        out_shape=pltpu.HBM((owners * slots, width), BF16),
        in_specs=[pl.BlockSpec(memory_space=pltpu.VMEM), pl.BlockSpec(memory_space=pltpu.HBM)],
        out_specs=pl.BlockSpec(memory_space=pltpu.HBM),
        scratch_shapes=[
            pltpu.VMEM((rows, width), BF16),
            pltpu.VMEM((owners * slots, rows), BF16),
            pltpu.VMEM((owners * slots, width), BF16),
            pltpu.SemaphoreType.DMA,
            pltpu.SemaphoreType.DMA((pieces,)),
        ],
        compiler_params=params(),
        cost_estimate=pl.CostEstimate(
            flops=2 * owners * slots * rows * width, bytes_accessed=5 * 10**6, transcendentals=0
        ),
        name="pick_rows",
    )(asked, in_hbm(table))


def prepare_kernel(block_ref, live_ref, weight_ref, seed_ref, self_ref, bias_ref, _, adj_ref, own_ref):
    seed_blocks, tiles, side, _ = weight_ref.shape
    slots = adj_ref.shape[1] // live_ref.shape[0]
    lane = lax.broadcasted_iota(jnp.int32, (side, side), 1)
    for b in range(seed_blocks):
        for k in range(tiles):
            block = block_ref[b, k]
            limit = jnp.where(lane < slots, live_ref[2 * block, 0], live_ref[2 * block + 1, 0] + slots)
            tile = jnp.where(lane < limit, weight_ref[b, k].astype(F32), 0.0)
            start = pl.multiple_of(block * side, side)
            adj_ref[b * side : (b + 1) * side, pl.ds(start, side)] = tile.astype(BF16)
    own_ref[...] = (
        jnp.dot(seed_ref[...], self_ref[...], preferred_element_type=F32) + bias_ref[...]
    )


def prepare(tile_block, live_count, tile_weight, seeds, self_weight, bias, after):
    seed_blocks, tiles, side, _ = tile_weight.shape
    targets, width = seeds.shape
    hidden = self_weight.shape[1]
    return pl.pallas_call(
        prepare_kernel,
        out_shape=(
            pltpu.HBM((seed_blocks * side, tiles * side), BF16),
            pltpu.HBM((targets, hidden), F32),
        ),
        in_specs=[
            pl.BlockSpec(memory_space=pltpu.SMEM),
            pl.BlockSpec(memory_space=pltpu.SMEM),
            pl.BlockSpec(memory_space=pltpu.VMEM),
            pl.BlockSpec(memory_space=pltpu.VMEM),
            pl.BlockSpec(memory_space=pltpu.VMEM),
            pl.BlockSpec(memory_space=pltpu.VMEM),
            pl.BlockSpec(memory_space=pl.ANY),
        ],
        out_specs=(pl.BlockSpec(memory_space=pltpu.VMEM), pl.BlockSpec(memory_space=pltpu.VMEM)),
        compiler_params=params(),
        cost_estimate=pl.CostEstimate(
            flops=2 * targets * width * hidden, bytes_accessed=6 * 10**6, transcendentals=0
        ),
        name="prepare",
    )(tile_block, live_count, tile_weight, seeds, self_weight, bias.reshape(1, -1), in_hbm(after))


def layer_kernel(
    core_ref, adj_hbm, rows_ref, neigh_hbm, own_hbm, cot_hbm, keep_ref, send_ref,
    adj_ref, neigh_ref, own_ref, cot_ref, agg_ref, out_ref, sems,
):
    pairs = [(adj_hbm, adj_ref), (neigh_hbm, neigh_ref), (own_hbm, own_ref), (cot_hbm, cot_ref)]
    loads = [pltpu.make_async_copy(src, dst, sems.at[i]) for i, (src, dst) in enumerate(pairs)]
    for load in loads:
        load.start()
    loads[0].wait()
    chunk = 256
    for start in range(0, rows_ref.shape[1], chunk):
        part = slice(start, start + chunk)
        agg = jnp.dot(adj_ref[...], rows_ref[:, part], preferred_element_type=F32)
        agg_ref[:, part] = agg.astype(BF16)
    for load in loads[1:]:
        load.wait()
    pre = own_ref[...] + jnp.dot(agg_ref[...], neigh_ref[...], preferred_element_type=F32)
    s = 1.0 / (1.0 + jnp.exp(-pre))
    slope = s * (1.0 + pre * (1.0 - s))
    grad = (cot_ref[...].astype(F32) * slope).astype(BF16)
    out_ref[...] = lax.dot_general(grad, agg_ref[...], (((0,), (0,)), ((), ())), preferred_element_type=F32)
    groups, span = keep_ref.shape[0], keep_ref.shape[1]

    def share(core):
        for x in range(groups):
            mine, other = (2 * x + core) * span, (2 * x + 1 - core) * span
            keep_ref[x] = out_ref[mine : mine + span, :]
            send_ref[x] = out_ref[other : other + span, :].astype(BF16)

    @pl.when(core_ref[0] == 0)
    def _():
        share(0)

    @pl.when(core_ref[0] == 1)
    def _():
        share(1)


def layer(core, adj, rows, neigh, own, cot, span):
    targets, fetched = adj.shape
    width, hidden = neigh.shape
    shape = (hidden // (2 * span), span, width)
    in_vmem, far = pl.BlockSpec(memory_space=pltpu.VMEM), pl.BlockSpec(memory_space=pltpu.HBM)
    return pl.pallas_call(
        layer_kernel,
        out_shape=(pltpu.VMEM(shape, F32), pltpu.VMEM(shape, BF16)),
        in_specs=[pl.BlockSpec(memory_space=pltpu.SMEM), far, in_vmem, far, far, far],
        out_specs=(in_vmem, in_vmem),
        scratch_shapes=[
            pltpu.VMEM((targets, fetched), BF16),
            pltpu.VMEM((width, hidden), BF16),
            pltpu.VMEM((targets, hidden), F32),
            pltpu.VMEM((targets, hidden), BF16),
            pltpu.VMEM((targets, width), BF16),
            pltpu.VMEM((hidden, width), F32),
            pltpu.SemaphoreType.DMA((4,)),
        ],
        compiler_params=params(),
        cost_estimate=pl.CostEstimate(
            flops=2 * targets * width * (fetched + 2 * hidden),
            bytes_accessed=8 * 10**6,
            transcendentals=targets * hidden,
        ),
        name="layer",
    )(core, in_hbm(adj), rows, in_hbm(neigh), in_hbm(own), in_hbm(cot))


def body(
    features,
    fetch_row,
    live_count,
    seed_features,
    tile_block,
    tile_weight,
    self_weight,
    neighbour_weight,
    layer_bias,
    cotangent,
):
    owners, slots = fetch_row.shape
    width, hidden = neighbour_weight.shape
    nx, nc, nz, ny = (lax.axis_size(a) for a in EVERY)
    span = hidden // (nx * nc)
    asked = lax.all_to_all(fetch_row.reshape(owners, 1, slots), GRP, split_axis=0, concat_axis=0, tiled=True)
    picked = pick_rows(asked, features)
    rows = lax.all_to_all(picked.reshape(owners, slots, width), GRP, split_axis=0, concat_axis=0, tiled=True)
    adj, own = prepare(tile_block, live_count, tile_weight, seed_features, self_weight, layer_bias, picked)
    core = lax.axis_index("c").astype(jnp.int32).reshape(1)
    keep, send = layer(core, adj, rows.reshape(owners * slots, width), neighbour_weight, own, cotangent, span)
    got = lax.ppermute(send, "c", [(0, 1), (1, 0)])
    pair = (keep + got.astype(F32)).astype(BF16)
    parts = lax.all_to_all(pair, "x", split_axis=0, concat_axis=0, tiled=True)
    ring = jnp.sum(parts.astype(F32), axis=0)
    cols = width // (nz * ny)
    pieces = ring.reshape(span, nz * ny, cols).transpose(1, 2, 0).reshape(nz * ny, cols * span)
    pieces = lax.all_to_all(pieces, REP, split_axis=0, concat_axis=0, tiled=True)
    return jnp.sum(pieces, axis=0).reshape(cols, span).T


def solution(mesh):
    n_grp, n_rep = mesh.shape["grp"], mesh.shape["rep"]
    chips, lines = n_grp // 2, int(round(n_rep**0.5))
    fine = Mesh(mesh.devices.reshape(chips, 2, lines, n_rep // lines), EVERY)
    placed = (
        P(EVERY, None),
        P(GRP, REP),
        P(GRP, REP),
        P(EVERY, None),
        P(EVERY, None),
        P(EVERY, None, None, None),
        P(),
        P(),
        P(),
        P(EVERY, None),
    )
    return jax.shard_map(body, mesh=fine, in_specs=placed, out_specs=P(GRP, REP), check_vma=False)
```

time: 129 us -> 123 us (0.953)
  local copies, waits for them, and re-layouts: 10.4 us -> 2.46 us
  Pallas kernels: 8.09 us -> 9.91 us
    unnamed x27 -> x13, local copies, waits for them, and re-layouts: 8.95 us -> 1.24 us
    pallas_call x3, Pallas kernels: 8.09 us -> 9.91 us  [the longest x1 4.16 us: layer(): pl.pallas_call(layer_kernel, out_shape=(pltpu.VMEM(shape, F32), pltpu.VME...]
  transfers between devices with their start and end apart: 2 -> 2, of which waited for: 2 -> 2; matrix products, arithmetic and copies ran while one was open for 0% -> 0% of each run, Pallas kernels for 1% -> 2%
where the time goes in v2:
time: 123 us
  blocking collectives  68 us (55%)
  waiting for transfers between devices  35.2 us (29%)
  Pallas kernels  9.91 us (8%)
  starting transfers between devices  6.77 us (6%)
  local copies, waits for them, and re-layouts  2.46 us (2%)
    all_to_all x1, blocking collectives, body(): lax.all_to_all(pieces, REP, split_axis=0, concat_axis=0, tiled=True)  34.8 us
    all_to_all x1, waiting for transfers between devices, body(): lax.all_to_all(picked.reshape(owners, slots, width), GRP, split_axis=0, c...  33.8 us
    all_to_all x1, blocking collectives, body(): parts = lax.all_to_all(pair, 'x', split_axis=0, concat_axis=0, tiled=True)  18.9 us
    all_to_all x1, blocking collectives, body(): lax.all_to_all(fetch_row.reshape(owners, 1, slots), GRP, split_axis=0, co...  14.4 us
    pallas_call x1, Pallas kernels, layer(): pl.pallas_call(layer_kernel, out_shape=(pltpu.VMEM(shape, F32), pltpu.VME...  4.16 us
    all_to_all x1, starting transfers between devices, body(): lax.all_to_all(picked.reshape(owners, slots, width), GRP, split_axis=0, c...  3.85 us
    pallas_call x1, Pallas kernels, pick_rows(): pl.pallas_call(pick_kernel, out_shape=pltpu.HBM((owners * slots, width),...  3.04 us
    ppermute x1, starting transfers between devices, body(): got = lax.ppermute(send, 'c', [(0, 1), (1, 0)])  2.92 us
  transfers between devices with their start and end apart: 2, of which 2 were waited for; matrix products, arithmetic and copies ran while one was open for 0% of the time, Pallas kernels for 2%

profile of v2, /device:TPU:16, one launch (start us, length us, event | category | flops | bytes accessed | tf_op | source)
XLA Modules:
  0.0 122.7 jit_solution(4535481356471341906)
XLA Ops:
  0.0 14.4 %all_to_all.24.asked_ref = s32[16,1,64]{2,1,0:T(1,128)S(1)} all-to-all(s32[16,1,64]{2,1,0:T(1,128)} %bitcast.15), channel_id=1, replica_groups=mesh['x'=8,'c'=2,'z'=8,'y'=8] {'x','c'}, dimensions={0} | all-to-all | bytes 8192 | tf_op jit(solution)/shard_map/all_to_all | solution.py:200
  14.4 3.0 %pick_rows.1._ = bf16[1024,768]{1,0:T(8,128)(2,1)} custom-call(s32[16,1,64]{2,1,0:T(1,128)S(1)} %all_to_all.24.asked_ref, bf16[512,768]{1,0:T(8,128)(2,1)} %table_ref.1), custom_call_target="tpu_custom_call" | custom-call | flops 805306368 | bytes 5000000 | tf_op jit(solution)/shard_map/pick_rows/pallas_call | solution.py:53
  17.4 0.0 copy-start.5
  17.4 0.0 copy-start
  17.4 0.0 copy-start.1
  17.5 0.0 copy-start.3
  17.5 0.0 copy-start.4
  17.5 3.9 %all-to-all-start.1 = ((bf16[16,64,768]{2,1,0:T(8,128)(2,1)}), bf16[16,64,768]{2,1,0:T(8,128)(2,1)S(1)}, u32[]{:S(2)}, u32[]{:S(2)}) async-start(bf16[16,64,768]{2,1,0:T(8,128)(2,1)} %bitcast.12), calls=%async_computation.1 | async-start | bytes 3145728 | tf_op jit(solution)/shard_map/all_to_all | solution.py:202
  21.3 0.0 copy-done.5
  21.3 0.1 copy.14.live_ref
  21.4 0.0 copy-done
  21.4 0.0 copy-done.1
  21.4 0.0 copy-done.3
  21.4 0.0 copy-done.4
  21.5 0.0 copy-start.2
  21.5 1.1 copy-done.2
  22.6 2.7 %prepare.1 = (bf16[512,1024]{1,0:T(8,128)(2,1)}, f32[512,512]{1,0:T(8,128)}) custom-call(s32[4,8]{1,0:T(4,128)S(1)} %copy-done.3, s32[16,1]{1,0:T(8,128)S(1)} %copy.14.live_ref, bf16[4,8,128,128]{3,2,1,0:T(8,128)(2,1)S(1)} %copy-done, bf16[512,768]{1,0:T(8,128)(2,1)S(1)} %copy-done.1, bf16[768,512]{1,0:T(8,128)(2,1)S(1)} %copy-done.2, ...), custom_call_target="tpu_custom_call" | custom-call | flops 402653184 | bytes 6000000 | tf_op jit(solution)/shard_map/prepare/pallas_call | solution.py:93
  25.3 33.8 %all-to-all-done.1 = bf16[16,64,768]{2,1,0:T(8,128)(2,1)S(1)} async-done(((bf16[16,64,768]{2,1,0:T(8,128)(2,1)}), bf16[16,64,768]{2,1,0:T(8,128)(2,1)S(1)}, u32[]{:S(2)}, u32[]{:S(2)}) %all-to-all-start.1) | async-done | bytes 1572896 | tf_op jit(solution)/shard_map/all_to_all | solution.py:202
  59.1 4.2 %layer.1 = (f32[8,32,768]{2,1,0:T(8,128)S(1)}, bf16[8,32,768]{2,1,0:T(8,128)(2,1)S(1)}) custom-call(s32[1]{0:T(128)} %bitcast.core_ref, bf16[512,1024]{1,0:T(8,128)(2,1)} %get-tuple-element.9.adj_hbm, bf16[1024,768]{1,0:T(8,128)(2,1)S(1)} %bitcast.10, bf16[768,512]{1,0:T(8,128)(2,1)} %neigh_hbm.1, f32[512,512]{1,0:T(8,128)} %get-tuple-element.10.own_hbm, ...), custom_call_target="tpu_custom_call" | custom-call | flops 1610612736 | bytes 8000000 | tf_op jit(solution)/shard_map/layer/pallas_call | solution.py:160
  63.3 2.9 %collective-permute-start = (bf16[8,32,768]{2,1,0:T(8,128)(2,1)S(1)}, bf16[8,32,768]{2,1,0:T(8,128)(2,1)S(1)}, u32[]{:S(2)}, u32[]{:S(2)}) collective-permute-start(bf16[8,32,768]{2,1,0:T(8,128)(2,1)S(1)} %get-tuple-element.12), channel_id=1, source_target_pairs={{0,64},{64,0},{1,65},{65,1},{2,66},{66,2},{3,67},{67,3},{4,68},{68... | collective-permute-start | bytes 1179656 | tf_op jit(solution)/shard_map/ppermute | solution.py:206
  66.2 1.3 %collective-permute-done = bf16[8,32,768]{2,1,0:T(8,128)(2,1)S(1)} collective-permute-done((bf16[8,32,768]{2,1,0:T(8,128)(2,1)S(1)}, bf16[8,32,768]{2,1,0:T(8,128)(2,1)S(1)}, u32[]{:S(2)}, u32[]{:S(2)}) %collective-permute-start) | collective-permute-done | bytes 393248 | tf_op jit(solution)/shard_map/ppermute | solution.py:206
  67.6 0.1 add_convert_fusion
  67.6 18.9 %all_to_all.25 = bf16[8,32,768]{2,1,0:T(8,128)(2,1)S(1)} all-to-all(bf16[8,32,768]{2,1,0:T(8,128)(2,1)S(1)} %add_convert_fusion), channel_id=1, replica_groups=mesh['x'=8,'c'=2,'z'=8,'y'=8] {'x'}, dimensions={0} | all-to-all | bytes 786432 | tf_op jit(solution)/shard_map/all_to_all | solution.py:208
  86.5 0.1 convert_reduce_fusion
  86.6 0.2 copy.15
  86.8 0.2 copy.16
  87.0 0.1 copy.17
  87.1 34.8 %all_to_all.26 = f32[64,1,384]{2,1,0:T(1,128)S(1)} all-to-all(f32[64,1,384]{2,1,0:T(1,128)S(1)} %copy.17), channel_id=1, replica_groups=mesh['x'=8,'c'=2,'z'=8,'y'=8] {'z','y'}, dimensions={0} | all-to-all | bytes 196608 | tf_op jit(solution)/shard_map/all_to_all | solution.py:212
  121.9 0.1 reduce_sum.19
  122.0 0.7 reshape.31
  (1 shorter events, 0.0 us)
Async XLA Ops:
  17.4 3.9 %copy-start.5 = (s32[16,1]{0,1:T(1,128)S(1)}, s32[16,1]{0,1:T(1,128)}, u32[]{:S(2)}) copy-start(s32[16,1]{0,1:T(1,128)} %param.12) | copy-start | bytes 196
  17.4 4.0 %copy-start = (bf16[4,8,128,128]{3,2,1,0:T(8,128)(2,1)S(1)}, bf16[4,8,128,128]{3,2,1,0:T(8,128)(2,1)}, u32[]{:S(2)}) copy-start(bf16[4,8,128,128]{3,2,1,0:T(8,128)(2,1)} %weight_ref.1) | copy-start | bytes 3145732
  17.4 4.0 %copy-start.1 = (bf16[512,768]{1,0:T(8,128)(2,1)S(1)}, bf16[512,768]{1,0:T(8,128)(2,1)}, u32[]{:S(2)}) copy-start(bf16[512,768]{1,0:T(8,128)(2,1)} %seed_ref.1) | copy-start | bytes 2359300
  17.5 4.0 %copy-start.3 = (s32[4,8]{1,0:T(4,128)S(1)}, s32[4,8]{1,0:T(4,128)}, u32[]{:S(2)}) copy-start(s32[4,8]{1,0:T(4,128)} %block_ref.1) | copy-start | bytes 388
  17.5 4.0 %copy-start.4 = (f32[512]{0:T(512)S(1)}, f32[512]{0:T(512)}, u32[]{:S(2)}) copy-start(f32[512]{0:T(512)} %param.18) | copy-start | bytes 6148
  17.5 41.7 %all-to-all-start.1 = ((bf16[16,64,768]{2,1,0:T(8,128)(2,1)}), bf16[16,64,768]{2,1,0:T(8,128)(2,1)S(1)}, u32[]{:S(2)}, u32[]{:S(2)}) async-start(bf16[16,64,768]{2,1,0:T(8,128)(2,1)} %bitcast.12), calls=%async_computation.1 | async-start | bytes 3145728 | tf_op jit(solution)/shard_map/all_to_all | solution.py:202
  21.5 1.1 copy-start.2
  63.3 4.3 %collective-permute-start = (bf16[8,32,768]{2,1,0:T(8,128)(2,1)S(1)}, bf16[8,32,768]{2,1,0:T(8,128)(2,1)S(1)}, u32[]{:S(2)}, u32[]{:S(2)}) collective-permute-start(bf16[8,32,768]{2,1,0:T(8,128)(2,1)S(1)} %get-tuple-element.12), channel_id=1, source_target_pairs={{0,64},{64,0},{1,65},{65,1},{2,66},{66,2},{3,67},{67,3},{4,68},{68... | collective-permute-start | bytes 1179656 | tf_op jit(solution)/shard_map/ppermute | solution.py:206

commit v3 on v2

v3 whole, which is shorter than its diff:
```python
import functools

import jax
import jax.numpy as jnp
from jax import lax
from jax.experimental import pallas as pl
from jax.experimental.pallas import tpu as pltpu
from jax.sharding import Mesh, PartitionSpec as P

F32 = jnp.float32
BF16 = jnp.bfloat16
GRP = ("x", "c")
REP = ("z", "y")
EVERY = GRP + REP
VMEM_LIMIT = 24 * 1024 * 1024


def in_hbm(array):
    return pltpu.with_memory_space_constraint(array, pltpu.HBM)


def params():
    return pltpu.CompilerParams(vmem_limit_bytes=VMEM_LIMIT)


def pick_kernel(asked_ref, table_ref, out_ref, table_buf, hot_ref, out_buf, table_sem, out_sems):
    owners, slots = asked_ref.shape[0], asked_ref.shape[2]
    rows = table_ref.shape[0]
    load = pltpu.make_async_copy(table_ref, table_buf, table_sem)
    load.start()
    line = lax.broadcasted_iota(jnp.int32, (slots, slots), 0)
    lane = lax.broadcasted_iota(jnp.int32, (slots, slots), 1)
    row_ix = lax.broadcasted_iota(jnp.int32, (slots, rows), 1).astype(F32)

    def build(first, last):
        for p in range(first, last):
            asked = jnp.broadcast_to(asked_ref[p].astype(F32), (slots, slots))
            column = jnp.sum(jnp.where(line == lane, asked, 0.0), axis=1, keepdims=True)
            hot_ref[p * slots : (p + 1) * slots, :] = jnp.where(row_ix == column, 1.0, 0.0).astype(BF16)

    pieces = out_sems.shape[0]
    each, early = owners // pieces, owners // 2
    size = each * slots
    build(0, early)
    load.wait()
    stores = []
    for i in range(pieces):
        build(max(i * each, early), max((i + 1) * each, early))
        part = pl.ds(i * size, size)
        out_buf[part, :] = jnp.dot(hot_ref[part, :], table_buf[...], preferred_element_type=F32).astype(BF16)
        stores.append(pltpu.make_async_copy(out_buf.at[part], out_ref.at[part], out_sems.at[i]))
        stores[i].start()
    for store in stores:
        store.wait()


def pick_rows(asked, table):
    owners, _, slots = asked.shape
    rows, width = table.shape
    pieces = 8
    return pl.pallas_call(
        pick_kernel,
        out_shape=pltpu.HBM((owners * slots, width), BF16),
        in_specs=[pl.BlockSpec(memory_space=pltpu.VMEM), pl.BlockSpec(memory_space=pltpu.HBM)],
        out_specs=pl.BlockSpec(memory_space=pltpu.HBM),
        scratch_shapes=[
            pltpu.VMEM((rows, width), BF16),
            pltpu.VMEM((owners * slots, rows), BF16),
            pltpu.VMEM((owners * slots, width), BF16),
            pltpu.SemaphoreType.DMA,
            pltpu.SemaphoreType.DMA((pieces,)),
        ],
        compiler_params=params(),
        cost_estimate=pl.CostEstimate(
            flops=2 * owners * slots * rows * width, bytes_accessed=5 * 10**6, transcendentals=0
        ),
        name="pick_rows",
    )(asked, in_hbm(table))


def core_major(array, span):
    starts = [(2 * x + core) * span for core in range(2) for x in range(array.shape[1] // (2 * span))]
    return jnp.concatenate([array[:, start : start + span] for start in starts], axis=1)


def prepare_kernel(
    span, block_ref, live_ref, weight_ref, seed_ref, self_ref, bias_ref, neigh_ref, cot_ref, _,
    adj_ref, own_ref, neigh_out, cot_out,
):
    seed_blocks, tiles, side, _ = weight_ref.shape
    slots = adj_ref.shape[1] // live_ref.shape[0]
    lane = lax.broadcasted_iota(jnp.int32, (side, side), 1)
    for b in range(seed_blocks):
        for k in range(tiles):
            block = block_ref[b, k]
            limit = jnp.where(lane < slots, live_ref[2 * block, 0], live_ref[2 * block + 1, 0] + slots)
            tile = jnp.where(lane < limit, weight_ref[b, k].astype(F32), 0.0)
            start = pl.multiple_of(block * side, side)
            adj_ref[b * side : (b + 1) * side, pl.ds(start, side)] = tile.astype(BF16)
    own = jnp.dot(seed_ref[...], self_ref[...], preferred_element_type=F32) + bias_ref[...]
    own_ref[...] = core_major(own, span)
    neigh_out[...] = core_major(neigh_ref[...], span)
    cot_out[...] = core_major(cot_ref[...], span)


def prepare(tile_block, live_count, tile_weight, seeds, self_weight, bias, neigh, cot, after, span):
    seed_blocks, tiles, side, _ = tile_weight.shape
    targets, width = seeds.shape
    hidden = self_weight.shape[1]
    near, far = pl.BlockSpec(memory_space=pltpu.VMEM), pl.BlockSpec(memory_space=pltpu.HBM)
    table = pl.BlockSpec(memory_space=pltpu.SMEM)
    return pl.pallas_call(
        functools.partial(prepare_kernel, span),
        out_shape=(
            pltpu.HBM((seed_blocks * side, tiles * side), BF16),
            pltpu.HBM((targets, hidden), F32),
            pltpu.HBM(neigh.shape, BF16),
            pltpu.HBM(cot.shape, BF16),
        ),
        in_specs=[table, table, near, near, near, near, near, near, far],
        out_specs=(near, near, near, near),
        compiler_params=params(),
        cost_estimate=pl.CostEstimate(
            flops=2 * targets * width * hidden, bytes_accessed=8 * 10**6, transcendentals=0
        ),
        name="prepare",
    )(tile_block, live_count, tile_weight, seeds, self_weight, bias.reshape(1, -1), neigh, cot, in_hbm(after))


def turned(left, right):
    return lax.dot_general(left, right, (((0,), (0,)), ((), ())), preferred_element_type=F32)


def layer_kernel(
    core_ref, adj_hbm, rows_ref, neigh_hbm, own_hbm, cot_hbm, send_ref, mine_ref, agg_ref,
    adj_ref, neigh_ref, own_ref, cot_ref, grad_ref, sems,
):
    pairs = [(adj_hbm, adj_ref), (neigh_hbm, neigh_ref), (own_hbm, own_ref), (cot_hbm, cot_ref)]
    loads = [pltpu.make_async_copy(src, dst, sems.at[i]) for i, (src, dst) in enumerate(pairs)]
    for load in loads:
        load.start()
    loads[0].wait()
    agg_ref[...] = jnp.dot(adj_ref[...], rows_ref[...], preferred_element_type=F32).astype(BF16)
    for load in loads[1:]:
        load.wait()
    targets, half = mine_ref.shape
    step = targets // 4
    for start in range(0, targets, step):
        part = slice(start, start + step)
        pre = own_ref[part, :] + jnp.dot(agg_ref[part, :], neigh_ref[...], preferred_element_type=F32)
        s = 1.0 / (1.0 + jnp.exp(-pre))
        slope = s * (1.0 + pre * (1.0 - s))
        grad_ref[part, :] = (cot_ref[part, :].astype(F32) * slope).astype(BF16)
    mine = pl.multiple_of(core_ref[0] * half, half)
    other = pl.multiple_of((1 - core_ref[0]) * half, half)
    mine_ref[...] = grad_ref[:, pl.ds(mine, half)]
    send_ref[...] = turned(grad_ref[:, pl.ds(other, half)], agg_ref[...]).astype(BF16)


def layer(core, adj, rows, neigh, own, cot):
    targets, fetched = adj.shape
    width, hidden = neigh.shape
    near, far = pl.BlockSpec(memory_space=pltpu.VMEM), pl.BlockSpec(memory_space=pltpu.HBM)
    return pl.pallas_call(
        layer_kernel,
        out_shape=(
            pltpu.VMEM((hidden // 2, width), BF16),
            pltpu.VMEM((targets, hidden // 2), BF16),
            pltpu.VMEM((targets, width), BF16),
        ),
        in_specs=[pl.BlockSpec(memory_space=pltpu.SMEM), far, near, far, far, far],
        out_specs=(near, near, near),
        scratch_shapes=[
            pltpu.VMEM((targets, fetched), BF16),
            pltpu.VMEM((width, hidden), BF16),
            pltpu.VMEM((targets, hidden), F32),
            pltpu.VMEM((targets, hidden), BF16),
            pltpu.VMEM((targets, hidden), BF16),
            pltpu.SemaphoreType.DMA((4,)),
        ],
        compiler_params=params(),
        cost_estimate=pl.CostEstimate(
            flops=2 * targets * width * (fetched + 2 * hidden),
            bytes_accessed=8 * 10**6,
            transcendentals=targets * hidden,
        ),
        name="layer",
    )(core, in_hbm(adj), rows, in_hbm(neigh), in_hbm(own), in_hbm(cot))


def own_term_kernel(mine_ref, agg_ref, keep_ref):
    keep_ref[...] = turned(mine_ref[...], agg_ref[...])


def own_term(mine, agg):
    targets, half = mine.shape
    width = agg.shape[1]
    near = pl.BlockSpec(memory_space=pltpu.VMEM)
    return pl.pallas_call(
        own_term_kernel,
        out_shape=pltpu.VMEM((half, width), F32),
        in_specs=[near, near],
        out_specs=near,
        compiler_params=params(),
        cost_estimate=pl.CostEstimate(
            flops=2 * targets * width * half, bytes_accessed=2 * 10**6, transcendentals=0
        ),
        name="own_term",
    )(mine, agg)


def body(
    features,
    fetch_row,
    live_count,
    seed_features,
    tile_block,
    tile_weight,
    self_weight,
    neighbour_weight,
    layer_bias,
    cotangent,
):
    owners, slots = fetch_row.shape
    width, hidden = neighbour_weight.shape
    nx, nc, nz, ny = (lax.axis_size(a) for a in EVERY)
    span = hidden // (nx * nc)
    asked = lax.all_to_all(fetch_row.reshape(owners, 1, slots), GRP, split_axis=0, concat_axis=0, tiled=True)
    picked = pick_rows(asked, features)
    rows = lax.all_to_all(picked.reshape(owners, slots, width), GRP, split_axis=0, concat_axis=0, tiled=True)
    adj, own, neigh, cot = prepare(
        tile_block, live_count, tile_weight, seed_features, self_weight, layer_bias, neighbour_weight, cotangent, picked, span
    )
    core = lax.axis_index("c").astype(jnp.int32).reshape(1)
    send, mine, agg = layer(core, adj, rows.reshape(owners * slots, width), neigh, own, cot)
    got = lax.ppermute(send, "c", [(0, 1), (1, 0)])
    keep = own_term(mine, agg)
    pair = (keep + got.astype(F32)).astype(BF16).reshape(nx, span, width)
    parts = lax.all_to_all(pair, "x", split_axis=0, concat_axis=0, tiled=True)
    ring = jnp.sum(parts.astype(F32), axis=0)
    cols = width // (nz * ny)
    pieces = ring.reshape(span, nz * ny, cols).transpose(1, 2, 0).reshape(nz * ny, cols * span)
    pieces = lax.all_to_all(pieces, REP, split_axis=0, concat_axis=0, tiled=True)
    return jnp.sum(pieces, axis=0).reshape(cols, span).T


def solution(mesh):
    n_grp, n_rep = mesh.shape["grp"], mesh.shape["rep"]
    chips, lines = n_grp // 2, int(round(n_rep**0.5))
    fine = Mesh(mesh.devices.reshape(chips, 2, lines, n_rep // lines), EVERY)
    placed = (
        P(EVERY, None),
        P(GRP, REP),
        P(GRP, REP),
        P(EVERY, None),
        P(EVERY, None),
        P(EVERY, None, None, None),
        P(),
        P(),
        P(),
        P(EVERY, None),
    )
    return jax.shard_map(body, mesh=fine, in_specs=placed, out_specs=P(GRP, REP), check_vma=False)
```

time: 123 us -> 123 us (level)
  waiting for transfers between devices: 35.2 us -> 31.1 us
  local copies, waits for them, and re-layouts: 2.46 us -> 4.63 us
  Pallas kernels: 9.91 us -> 11.3 us
    all_to_all x1, waiting for transfers between devices: 33.8 us -> 30.2 us  [body(): lax.all_to_all(picked.reshape(owners, slots, width), GRP, split_axis=0, c...]
    unnamed x13 -> x17, local copies, waits for them, and re-layouts: 1.24 us -> 3.42 us
    pallas_call x2 -> x3, Pallas kernels: 6.87 us -> 8.44 us  [the longest x1 4.17 us: prepare(): pl.pallas_call(functools.partial(prepare_kernel, span), out_shape=(pltpu....]
  transfers between devices with their start and end apart: 2 -> 2, of which waited for: 2 -> 2; matrix products, arithmetic and copies ran while one was open for 0% -> 0% of each run, Pallas kernels for 2% -> 4%
where the time goes in v3:
time: 123 us; the launch traced here: 122 us
  blocking collectives  68 us (55%)
  waiting for transfers between devices  31.1 us (25%)
  Pallas kernels  11.3 us (9%)
  starting transfers between devices  6.71 us (5%)
  local copies, waits for them, and re-layouts  4.63 us (4%)
    all_to_all x1, blocking collectives, body(): lax.all_to_all(pieces, REP, split_axis=0, concat_axis=0, tiled=True)  34.8 us
    all_to_all x1, waiting for transfers between devices, body(): lax.all_to_all(picked.reshape(owners, slots, width), GRP, split_axis=0, c...  30.2 us
    all_to_all x1, blocking collectives, body(): parts = lax.all_to_all(pair, 'x', split_axis=0, concat_axis=0, tiled=True)  18.9 us
    all_to_all x1, blocking collectives, body(): lax.all_to_all(fetch_row.reshape(owners, 1, slots), GRP, split_axis=0, co...  14.4 us
    pallas_call x1, Pallas kernels, prepare(): pl.pallas_call(functools.partial(prepare_kernel, span), out_shape=(pltpu....  4.17 us
    pallas_call x1, Pallas kernels, layer(): pl.pallas_call(layer_kernel, out_shape=(pltpu.VMEM((hidden // 2, width),...  3.86 us
    all_to_all x1, starting transfers between devices, body(): lax.all_to_all(picked.reshape(owners, slots, width), GRP, split_axis=0, c...  3.85 us
    unnamed x17, local copies, waits for them, and re-layouts  3.42 us
  transfers between devices with their start and end apart: 2, of which 2 were waited for; matrix products, arithmetic and copies ran while one was open for 0% of the time, Pallas kernels for 4%

profile of v3, /device:TPU:16, one launch (start us, length us, event | category | flops | bytes accessed | tf_op | source)
XLA Modules:
  0.0 122.2 jit_solution(1199893422055347724)
XLA Ops:
  0.0 14.4 %all_to_all.24.asked_ref = s32[16,1,64]{2,1,0:T(1,128)S(1)} all-to-all(s32[16,1,64]{2,1,0:T(1,128)} %bitcast.17), channel_id=1, replica_groups=mesh['x'=8,'c'=2,'z'=8,'y'=8] {'x','c'}, dimensions={0} | all-to-all | bytes 8192 | tf_op jit(solution)/shard_map/all_to_all | solution.py:228
  14.4 2.9 %pick_rows.1._ = bf16[1024,768]{1,0:T(8,128)(2,1)} custom-call(s32[16,1,64]{2,1,0:T(1,128)S(1)} %all_to_all.24.asked_ref, bf16[512,768]{1,0:T(8,128)(2,1)} %table_ref.1), custom_call_target="tpu_custom_call" | custom-call | flops 805306368 | bytes 5000000 | tf_op jit(solution)/shard_map/pick_rows/pallas_call | solution.py:61
  17.3 0.0 copy-start.7
  17.3 0.0 copy-start
  17.3 0.0 copy-start.1
  17.3 0.0 copy-start.5
  17.3 0.0 copy-start.6
  17.3 3.9 %all-to-all-start.1 = ((bf16[16,64,768]{2,1,0:T(8,128)(2,1)}), bf16[16,64,768]{2,1,0:T(8,128)(2,1)S(1)}, u32[]{:S(2)}, u32[]{:S(2)}) async-start(bf16[16,64,768]{2,1,0:T(8,128)(2,1)} %bitcast.13), calls=%async_computation.1 | async-start | bytes 3145728 | tf_op jit(solution)/shard_map/all_to_all | solution.py:230
  21.2 0.0 copy-done.7
  21.2 0.1 copy.14.live_ref
  21.3 0.0 copy-done
  21.3 0.0 copy-done.1
  21.3 0.0 copy-done.5
  21.3 0.0 copy-done.6
  21.3 0.0 copy-start.2
  21.3 1.1 copy-done.2
  22.4 0.0 copy-start.3
  22.4 1.1 copy-done.3
  23.6 0.0 copy-start.4
  23.6 1.0 copy-done.4
  24.6 4.2 %prepare.1 = (bf16[512,1024]{1,0:T(8,128)(2,1)}, f32[512,512]{1,0:T(8,128)}, bf16[768,512]{1,0:T(8,128)(2,1)}, bf16[512,512]{1,0:T(8,128)(2,1)}) custom-call(s32[4,8]{1,0:T(4,128)S(1)} %copy-done.5, s32[16,1]{1,0:T(8,128)S(1)} %copy.14.live_ref, bf16[4,8,128,128]{3,2,1,0:T(8,128)(2,1)S(1)} %copy-done, bf16[512,768]{1,0:T(8,128)(2,1)S(1)} %copy-done.1, ...), custom_call_target="tpu_custom_call" | custom-call | flops 402653184 | bytes 8000000 | tf_op jit(solution)/shard_map/prepare/pallas_call | solution.py:112
  28.8 30.2 %all-to-all-done.1 = bf16[16,64,768]{2,1,0:T(8,128)(2,1)S(1)} async-done(((bf16[16,64,768]{2,1,0:T(8,128)(2,1)}), bf16[16,64,768]{2,1,0:T(8,128)(2,1)S(1)}, u32[]{:S(2)}, u32[]{:S(2)}) %all-to-all-start.1) | async-done | bytes 1572896 | tf_op jit(solution)/shard_map/all_to_all | solution.py:230
  59.0 3.9 %layer.1 = (bf16[256,768]{1,0:T(8,128)(2,1)S(1)}, bf16[512,256]{1,0:T(8,128)(2,1)S(1)}, bf16[512,768]{1,0:T(8,128)(2,1)S(1)}) custom-call(s32[1]{0:T(128)} %bitcast.core_ref, bf16[512,1024]{1,0:T(8,128)(2,1)} %get-tuple-element.12.adj_hbm, bf16[1024,768]{1,0:T(8,128)(2,1)S(1)} %bitcast.11, bf16[768,512]{1,0:T(8,128)(2,1)} %get-tuple-element.13.neigh_hbm, ...), custom_call_target="tpu_custom_call" | custom-call | flops 1610612736 | bytes 8000000 | tf_op jit(solution)/shard_map/layer/pallas_call | solution.py:164
  62.9 2.9 %collective-permute-start = (bf16[256,768]{1,0:T(8,128)(2,1)S(1)}, bf16[256,768]{1,0:T(8,128)(2,1)S(1)}, u32[]{:S(2)}, u32[]{:S(2)}) collective-permute-start(bf16[256,768]{1,0:T(8,128)(2,1)S(1)} %get-tuple-element.18), channel_id=1, source_target_pairs={{0,64},{64,0},{1,65},{65,1},{2,66},{66,2},{3,67},{67,3},{4,68},{68... | collective-permute-start | bytes 1179656 | tf_op jit(solution)/shard_map/ppermute | solution.py:236
  65.7 0.4 own_term.1
  66.1 0.9 collective-permute-done
  67.1 0.1 add_convert_fusion
  67.1 18.9 %all_to_all.25 = bf16[8,32,768]{2,1,0:T(8,128)(2,1)S(1)} all-to-all(bf16[8,32,768]{2,1,0:T(8,128)(2,1)S(1)} %bitcast.15), channel_id=1, replica_groups=mesh['x'=8,'c'=2,'z'=8,'y'=8] {'x'}, dimensions={0} | all-to-all | bytes 786432 | tf_op jit(solution)/shard_map/all_to_all | solution.py:239
  86.0 0.1 convert_reduce_fusion
  86.1 0.2 copy.15
  86.3 0.2 copy.16
  86.5 0.1 copy.17
  86.6 34.8 %all_to_all.26 = f32[64,1,384]{2,1,0:T(1,128)S(1)} all-to-all(f32[64,1,384]{2,1,0:T(1,128)S(1)} %copy.17), channel_id=1, replica_groups=mesh['x'=8,'c'=2,'z'=8,'y'=8] {'z','y'}, dimensions={0} | all-to-all | bytes 196608 | tf_op jit(solution)/shard_map/all_to_all | solution.py:243
  121.4 0.1 reduce_sum.19
  121.5 0.7 reshape.35
  (1 shorter events, 0.0 us)
Async XLA Ops:
  17.3 3.9 %copy-start.7 = (s32[16,1]{0,1:T(1,128)S(1)}, s32[16,1]{0,1:T(1,128)}, u32[]{:S(2)}) copy-start(s32[16,1]{0,1:T(1,128)} %param.12) | copy-start | bytes 196
  17.3 4.0 %copy-start = (bf16[4,8,128,128]{3,2,1,0:T(8,128)(2,1)S(1)}, bf16[4,8,128,128]{3,2,1,0:T(8,128)(2,1)}, u32[]{:S(2)}) copy-start(bf16[4,8,128,128]{3,2,1,0:T(8,128)(2,1)} %weight_ref.1) | copy-start | bytes 3145732
  17.3 4.0 %copy-start.1 = (bf16[512,768]{1,0:T(8,128)(2,1)S(1)}, bf16[512,768]{1,0:T(8,128)(2,1)}, u32[]{:S(2)}) copy-start(bf16[512,768]{1,0:T(8,128)(2,1)} %seed_ref.1) | copy-start | bytes 2359300
  17.3 4.0 %copy-start.5 = (s32[4,8]{1,0:T(4,128)S(1)}, s32[4,8]{1,0:T(4,128)}, u32[]{:S(2)}) copy-start(s32[4,8]{1,0:T(4,128)} %block_ref.1) | copy-start | bytes 388
  17.3 4.0 %copy-start.6 = (f32[512]{0:T(512)S(1)}, f32[512]{0:T(512)}, u32[]{:S(2)}) copy-start(f32[512]{0:T(512)} %param.18) | copy-start | bytes 6148
  17.3 41.7 %all-to-all-start.1 = ((bf16[16,64,768]{2,1,0:T(8,128)(2,1)}), bf16[16,64,768]{2,1,0:T(8,128)(2,1)S(1)}, u32[]{:S(2)}, u32[]{:S(2)}) async-start(bf16[16,64,768]{2,1,0:T(8,128)(2,1)} %bitcast.13), calls=%async_computation.1 | async-start | bytes 3145728 | tf_op jit(solution)/shard_map/all_to_all | solution.py:230
  21.3 1.1 copy-start.2
  22.4 1.1 copy-start.3
  23.6 1.0 copy-start.4
  62.9 4.2 %collective-permute-start = (bf16[256,768]{1,0:T(8,128)(2,1)S(1)}, bf16[256,768]{1,0:T(8,128)(2,1)S(1)}, u32[]{:S(2)}, u32[]{:S(2)}) collective-permute-start(bf16[256,768]{1,0:T(8,128)(2,1)S(1)} %get-tuple-element.18), channel_id=1, source_target_pairs={{0,64},{64,0},{1,65},{65,1},{2,66},{66,2},{3,67},{67,3},{4,68},{68... | collective-permute-start | bytes 1179656 | tf_op jit(solution)/shard_map/ppermute | solution.py:236

commit v4 on v3

--- a/solution.py
+++ b/solution.py
@@ -15,6 +15,10 @@
 VMEM_LIMIT = 24 * 1024 * 1024
 
 
+def in_vmem(array):
+    return pltpu.with_memory_space_constraint(array, pltpu.VMEM)
+
+
 def in_hbm(array):
     return pltpu.with_memory_space_constraint(array, pltpu.HBM)
 
@@ -23,11 +27,9 @@
     return pltpu.CompilerParams(vmem_limit_bytes=VMEM_LIMIT)
 
 
-def pick_kernel(asked_ref, table_ref, out_ref, table_buf, hot_ref, out_buf, table_sem, out_sems):
+def pick_kernel(asked_ref, table_ref, out_ref, hot_ref, out_buf, out_sems):
     owners, slots = asked_ref.shape[0], asked_ref.shape[2]
     rows = table_ref.shape[0]
-    load = pltpu.make_async_copy(table_ref, table_buf, table_sem)
-    load.start()
     line = lax.broadcasted_iota(jnp.int32, (slots, slots), 0)
     lane = lax.broadcasted_iota(jnp.int32, (slots, slots), 1)
     row_ix = lax.broadcasted_iota(jnp.int32, (slots, rows), 1).astype(F32)
@@ -42,18 +44,36 @@
     each, early = owners // pieces, owners // 2
     size = each * slots
     build(0, early)
-    load.wait()
     stores = []
     for i in range(pieces):
         build(max(i * each, early), max((i + 1) * each, early))
         part = pl.ds(i * size, size)
-        out_buf[part, :] = jnp.dot(hot_ref[part, :], table_buf[...], preferred_element_type=F32).astype(BF16)
+        out_buf[part, :] = jnp.dot(hot_ref[part, :], table_ref[...], preferred_element_type=F32).astype(BF16)
         stores.append(pltpu.make_async_copy(out_buf.at[part], out_ref.at[part], out_sems.at[i]))
         stores[i].start()
     for store in stores:
         store.wait()
 
 
+def stage_kernel(table_ref, out_ref, sem):
+    load = pltpu.make_async_copy(table_ref, out_ref, sem)
+    load.start()
+    load.wait()
+
+
+def stage(table):
+    return pl.pallas_call(
+        stage_kernel,
+        out_shape=pltpu.VMEM(table.shape, table.dtype),
+        in_specs=[pl.BlockSpec(memory_space=pltpu.HBM)],
+        out_specs=pl.BlockSpec(memory_space=pltpu.VMEM),
+        scratch_shapes=[pltpu.SemaphoreType.DMA],
+        compiler_params=params(),
+        cost_estimate=pl.CostEstimate(flops=0, bytes_accessed=2 * 10**6, transcendentals=0),
+        name="stage",
+    )(in_hbm(table))
+
+
 def pick_rows(asked, table):
     owners, _, slots = asked.shape
     rows, width = table.shape
@@ -61,13 +81,11 @@
     return pl.pallas_call(
         pick_kernel,
         out_shape=pltpu.HBM((owners * slots, width), BF16),
-        in_specs=[pl.BlockSpec(memory_space=pltpu.VMEM), pl.BlockSpec(memory_space=pltpu.HBM)],
+        in_specs=[pl.BlockSpec(memory_space=pltpu.VMEM), pl.BlockSpec(memory_space=pltpu.VMEM)],
         out_specs=pl.BlockSpec(memory_space=pltpu.HBM),
         scratch_shapes=[
-            pltpu.VMEM((rows, width), BF16),
             pltpu.VMEM((owners * slots, rows), BF16),
             pltpu.VMEM((owners * slots, width), BF16),
-            pltpu.SemaphoreType.DMA,
             pltpu.SemaphoreType.DMA((pieces,)),
         ],
         compiler_params=params(),
@@ -75,7 +93,7 @@
             flops=2 * owners * slots * rows * width, bytes_accessed=5 * 10**6, transcendentals=0
         ),
         name="pick_rows",
-    )(asked, in_hbm(table))
+    )(asked, in_vmem(table))
 
 
 def core_major(array, span):
@@ -226,7 +244,7 @@
     nx, nc, nz, ny = (lax.axis_size(a) for a in EVERY)
     span = hidden // (nx * nc)
     asked = lax.all_to_all(fetch_row.reshape(owners, 1, slots), GRP, split_axis=0, concat_axis=0, tiled=True)
-    picked = pick_rows(asked, features)
+    picked = pick_rows(asked, stage(features))
     rows = lax.all_to_all(picked.reshape(owners, slots, width), GRP, split_axis=0, concat_axis=0, tiled=True)
     adj, own, neigh, cot = prepare(
         tile_block, live_count, tile_weight, seed_features, self_weight, layer_bias, neighbour_weight, cotangent, picked, span

time: 123 us -> 122 us (level)
  blocking collectives: 68 us -> 53.7 us
  starting transfers between devices: 6.71 us -> 13.6 us
  waiting for transfers between devices: 31.1 us -> 37.5 us
    all_to_all x1 -> x0, blocking collectives: 14.4 us -> none  [body(): lax.all_to_all(fetch_row.reshape(owners, 1, slots), GRP, split_axis=0, co...]
    all_to_all x0 -> x1, starting transfers between devices: none -> 6.86 us  [body(): lax.all_to_all(fetch_row.reshape(owners, 1, slots), GRP, split_axis=0, co...]
    all_to_all x0 -> x1, waiting for transfers between devices: none -> 6.35 us  [body(): lax.all_to_all(fetch_row.reshape(owners, 1, slots), GRP, split_axis=0, co...]
  transfers between devices with their start and end apart: 2 -> 3, of which waited for: 2 -> 3; matrix products, arithmetic and copies ran while one was open for 0% -> 0% of each run, Pallas kernels for 4% -> 5%
where the time goes in v4:
time: 122 us; the launch traced here: 121 us
  blocking collectives  53.7 us (44%)
  waiting for transfers between devices  37.5 us (31%)
  starting transfers between devices  13.6 us (11%)
  Pallas kernels  11.4 us (9%)
  local copies, waits for them, and re-layouts  4.63 us (4%)
    all_to_all x1, blocking collectives, body(): lax.all_to_all(pieces, REP, split_axis=0, concat_axis=0, tiled=True)  34.8 us
    all_to_all x1, waiting for transfers between devices, body(): lax.all_to_all(picked.reshape(owners, slots, width), GRP, split_axis=0, c...  30.2 us
    all_to_all x1, blocking collectives, body(): parts = lax.all_to_all(pair, 'x', split_axis=0, concat_axis=0, tiled=True)  18.9 us
    all_to_all x1, starting transfers between devices, body(): lax.all_to_all(fetch_row.reshape(owners, 1, slots), GRP, split_axis=0, co...  6.86 us
    all_to_all x1, waiting for transfers between devices, body(): lax.all_to_all(fetch_row.reshape(owners, 1, slots), GRP, split_axis=0, co...  6.35 us
    pallas_call x1, Pallas kernels, prepare(): pl.pallas_call(functools.partial(prepare_kernel, span), out_shape=(pltpu....  4.15 us
    pallas_call x1, Pallas kernels, layer(): pl.pallas_call(layer_kernel, out_shape=(pltpu.VMEM((hidden // 2, width),...  3.86 us
    all_to_all x1, starting transfers between devices, body(): lax.all_to_all(picked.reshape(owners, slots, width), GRP, split_axis=0, c...  3.85 us
  transfers between devices with their start and end apart: 3, of which 3 were waited for; matrix products, arithmetic and copies ran while one was open for 0% of the time, Pallas kernels for 5%

profile of v4, /device:TPU:16, one launch (start us, length us, event | category | flops | bytes accessed | tf_op | source)
XLA Modules:
  0.0 121.2 jit_solution(12617974776295625531)
XLA Ops:
  0.0 6.9 %all-to-all-start = ((s32[16,1,64]{2,1,0:T(1,128)}), s32[16,1,64]{2,1,0:T(1,128)S(1)}, u32[]{:S(2)}, u32[]{:S(2)}) async-start(s32[16,1,64]{2,1,0:T(1,128)} %bitcast.17), calls=%async_computation | async-start | bytes 16384 | tf_op jit(solution)/shard_map/all_to_all | solution.py:246
  6.9 1.1 stage.1.table_ref
  8.0 6.3 %all-to-all-done.asked_ref = s32[16,1,64]{2,1,0:T(1,128)S(1)} async-done(((s32[16,1,64]{2,1,0:T(1,128)}), s32[16,1,64]{2,1,0:T(1,128)S(1)}, u32[]{:S(2)}, u32[]{:S(2)}) %all-to-all-start) | async-done | bytes 4128 | tf_op jit(solution)/shard_map/all_to_all | solution.py:246
  14.4 1.8 %pick_rows.1._ = bf16[1024,768]{1,0:T(8,128)(2,1)} custom-call(s32[16,1,64]{2,1,0:T(1,128)S(1)} %all-to-all-done.asked_ref, bf16[512,768]{1,0:T(8,128)(2,1)S(1)} %stage.1.table_ref), custom_call_target="tpu_custom_call" | custom-call | flops 805306368 | bytes 5000000 | tf_op jit(solution)/shard_map/pick_rows/pallas_call | solution.py:81
  16.2 0.0 copy-start.7
  16.2 0.0 copy-start
  16.2 0.0 copy-start.1
  16.3 0.0 copy-start.5
  16.3 0.0 copy-start.6
  16.3 3.9 %all-to-all-start.1 = ((bf16[16,64,768]{2,1,0:T(8,128)(2,1)}), bf16[16,64,768]{2,1,0:T(8,128)(2,1)S(1)}, u32[]{:S(2)}, u32[]{:S(2)}) async-start(bf16[16,64,768]{2,1,0:T(8,128)(2,1)} %bitcast.13), calls=%async_computation.1 | async-start | bytes 3145728 | tf_op jit(solution)/shard_map/all_to_all | solution.py:248
  20.1 0.0 copy-done.7
  20.1 0.1 copy.14.live_ref
  20.2 0.0 copy-done
  20.2 0.0 copy-done.1
  20.2 0.0 copy-done.5
  20.2 0.0 copy-done.6
  20.3 0.0 copy-start.2
  20.3 1.1 copy-done.2
  21.4 0.0 copy-start.3
  21.4 1.1 copy-done.3
  22.5 0.0 copy-start.4
  22.5 1.0 copy-done.4
  23.6 4.2 %prepare.1 = (bf16[512,1024]{1,0:T(8,128)(2,1)}, f32[512,512]{1,0:T(8,128)}, bf16[768,512]{1,0:T(8,128)(2,1)}, bf16[512,512]{1,0:T(8,128)(2,1)}) custom-call(s32[4,8]{1,0:T(4,128)S(1)} %copy-done.5, s32[16,1]{1,0:T(8,128)S(1)} %copy.14.live_ref, bf16[4,8,128,128]{3,2,1,0:T(8,128)(2,1)S(1)} %copy-done, bf16[512,768]{1,0:T(8,128)(2,1)S(1)} %copy-done.1, ...), custom_call_target="tpu_custom_call" | custom-call | flops 402653184 | bytes 8000000 | tf_op jit(solution)/shard_map/prepare/pallas_call | solution.py:130
  27.7 30.2 %all-to-all-done.1 = bf16[16,64,768]{2,1,0:T(8,128)(2,1)S(1)} async-done(((bf16[16,64,768]{2,1,0:T(8,128)(2,1)}), bf16[16,64,768]{2,1,0:T(8,128)(2,1)S(1)}, u32[]{:S(2)}, u32[]{:S(2)}) %all-to-all-start.1) | async-done | bytes 1572896 | tf_op jit(solution)/shard_map/all_to_all | solution.py:248
  57.9 3.9 %layer.1 = (bf16[256,768]{1,0:T(8,128)(2,1)S(1)}, bf16[512,256]{1,0:T(8,128)(2,1)S(1)}, bf16[512,768]{1,0:T(8,128)(2,1)S(1)}) custom-call(s32[1]{0:T(128)} %bitcast.core_ref, bf16[512,1024]{1,0:T(8,128)(2,1)} %get-tuple-element.12.adj_hbm, bf16[1024,768]{1,0:T(8,128)(2,1)S(1)} %bitcast.11, bf16[768,512]{1,0:T(8,128)(2,1)} %get-tuple-element.13.neigh_hbm, ...), custom_call_target="tpu_custom_call" | custom-call | flops 1610612736 | bytes 8000000 | tf_op jit(solution)/shard_map/layer/pallas_call | solution.py:182
  61.8 2.9 %collective-permute-start = (bf16[256,768]{1,0:T(8,128)(2,1)S(1)}, bf16[256,768]{1,0:T(8,128)(2,1)S(1)}, u32[]{:S(2)}, u32[]{:S(2)}) collective-permute-start(bf16[256,768]{1,0:T(8,128)(2,1)S(1)} %get-tuple-element.18), channel_id=1, source_target_pairs={{0,64},{64,0},{1,65},{65,1},{2,66},{66,2},{3,67},{67,3},{4,68},{68... | collective-permute-start | bytes 1179656 | tf_op jit(solution)/shard_map/ppermute | solution.py:254
  64.7 0.4 own_term.1
  65.1 0.9 collective-permute-done
  66.0 0.1 add_convert_fusion
  66.1 18.9 %all_to_all.24 = bf16[8,32,768]{2,1,0:T(8,128)(2,1)S(1)} all-to-all(bf16[8,32,768]{2,1,0:T(8,128)(2,1)S(1)} %bitcast.15), channel_id=1, replica_groups=mesh['x'=8,'c'=2,'z'=8,'y'=8] {'x'}, dimensions={0} | all-to-all | bytes 786432 | tf_op jit(solution)/shard_map/all_to_all | solution.py:257
  85.0 0.1 convert_reduce_fusion
  85.0 0.2 copy.15
  85.3 0.2 copy.16
  85.5 0.1 copy.17
  85.6 34.8 %all_to_all.25 = f32[64,1,384]{2,1,0:T(1,128)S(1)} all-to-all(f32[64,1,384]{2,1,0:T(1,128)S(1)} %copy.17), channel_id=1, replica_groups=mesh['x'=8,'c'=2,'z'=8,'y'=8] {'z','y'}, dimensions={0} | all-to-all | bytes 196608 | tf_op jit(solution)/shard_map/all_to_all | solution.py:261
  120.4 0.1 reduce_sum.19
  120.5 0.7 reshape.35
  (1 shorter events, 0.0 us)
Async XLA Ops:
  0.0 14.4 %all-to-all-start = ((s32[16,1,64]{2,1,0:T(1,128)}), s32[16,1,64]{2,1,0:T(1,128)S(1)}, u32[]{:S(2)}, u32[]{:S(2)}) async-start(s32[16,1,64]{2,1,0:T(1,128)} %bitcast.17), calls=%async_computation | async-start | bytes 16384 | tf_op jit(solution)/shard_map/all_to_all | solution.py:246
  16.2 3.9 %copy-start.7 = (s32[16,1]{0,1:T(1,128)S(1)}, s32[16,1]{0,1:T(1,128)}, u32[]{:S(2)}) copy-start(s32[16,1]{0,1:T(1,128)} %param.12) | copy-start | bytes 196
  16.2 4.0 %copy-start = (bf16[4,8,128,128]{3,2,1,0:T(8,128)(2,1)S(1)}, bf16[4,8,128,128]{3,2,1,0:T(8,128)(2,1)}, u32[]{:S(2)}) copy-start(bf16[4,8,128,128]{3,2,1,0:T(8,128)(2,1)} %weight_ref.1) | copy-start | bytes 3145732
  16.2 4.0 %copy-start.1 = (bf16[512,768]{1,0:T(8,128)(2,1)S(1)}, bf16[512,768]{1,0:T(8,128)(2,1)}, u32[]{:S(2)}) copy-start(bf16[512,768]{1,0:T(8,128)(2,1)} %seed_ref.1) | copy-start | bytes 2359300
  16.3 4.0 %copy-start.5 = (s32[4,8]{1,0:T(4,128)S(1)}, s32[4,8]{1,0:T(4,128)}, u32[]{:S(2)}) copy-start(s32[4,8]{1,0:T(4,128)} %block_ref.1) | copy-start | bytes 388
  16.3 4.0 %copy-start.6 = (f32[512]{0:T(512)S(1)}, f32[512]{0:T(512)}, u32[]{:S(2)}) copy-start(f32[512]{0:T(512)} %param.18) | copy-start | bytes 6148
  16.3 41.7 %all-to-all-start.1 = ((bf16[16,64,768]{2,1,0:T(8,128)(2,1)}), bf16[16,64,768]{2,1,0:T(8,128)(2,1)S(1)}, u32[]{:S(2)}, u32[]{:S(2)}) async-start(bf16[16,64,768]{2,1,0:T(8,128)(2,1)} %bitcast.13), calls=%async_computation.1 | async-start | bytes 3145728 | tf_op jit(solution)/shard_map/all_to_all | solution.py:248
  20.3 1.1 copy-start.2
  21.4 1.1 copy-start.3
  22.5 1.0 copy-start.4
  61.8 4.2 %collective-permute-start = (bf16[256,768]{1,0:T(8,128)(2,1)S(1)}, bf16[256,768]{1,0:T(8,128)(2,1)S(1)}, u32[]{:S(2)}, u32[]{:S(2)}) collective-permute-start(bf16[256,768]{1,0:T(8,128)(2,1)S(1)} %get-tuple-element.18), channel_id=1, source_target_pairs={{0,64},{64,0},{1,65},{65,1},{2,66},{66,2},{3,67},{67,3},{4,68},{68... | collective-permute-start | bytes 1179656 | tf_op jit(solution)/shard_map/ppermute | solution.py:254

commit v5 on v4

v5 whole, which is shorter than its diff:
```python
import functools

import jax
import jax.numpy as jnp
from jax import lax
from jax.experimental import pallas as pl
from jax.experimental.pallas import tpu as pltpu
from jax.sharding import Mesh, PartitionSpec as P

F32 = jnp.float32
BF16 = jnp.bfloat16
GRP = ("x", "c")
REP = ("z", "y")
EVERY = GRP + REP
VMEM_LIMIT = 24 * 1024 * 1024


def in_vmem(array):
    return pltpu.with_memory_space_constraint(array, pltpu.VMEM)


def in_hbm(array):
    return pltpu.with_memory_space_constraint(array, pltpu.HBM)


def params():
    return pltpu.CompilerParams(vmem_limit_bytes=VMEM_LIMIT)


def pick_kernel(asked_ref, table_ref, out_ref, hot_ref, out_buf, out_sems):
    owners, slots = asked_ref.shape[0], asked_ref.shape[2]
    rows = table_ref.shape[0]
    line = lax.broadcasted_iota(jnp.int32, (slots, slots), 0)
    lane = lax.broadcasted_iota(jnp.int32, (slots, slots), 1)
    row_ix = lax.broadcasted_iota(jnp.int32, (slots, rows), 1).astype(F32)

    def build(first, last):
        for p in range(first, last):
            asked = jnp.broadcast_to(asked_ref[p].astype(F32), (slots, slots))
            column = jnp.sum(jnp.where(line == lane, asked, 0.0), axis=1, keepdims=True)
            hot_ref[p * slots : (p + 1) * slots, :] = jnp.where(row_ix == column, 1.0, 0.0).astype(BF16)

    pieces = out_sems.shape[0]
    each, early = owners // pieces, owners // 2
    size = each * slots
    build(0, early)
    stores = []
    for i in range(pieces):
        build(max(i * each, early), max((i + 1) * each, early))
        part = pl.ds(i * size, size)
        out_buf[part, :] = jnp.dot(hot_ref[part, :], table_ref[...], preferred_element_type=F32).astype(BF16)
        stores.append(pltpu.make_async_copy(out_buf.at[part], out_ref.at[part], out_sems.at[i]))
        stores[i].start()
    for store in stores:
        store.wait()


def stage_kernel(
    block_ref, live_ref, weight_hbm, table_hbm, seed_hbm, self_hbm, bias_ref, adj_hbm, own_hbm, table_ref,
    weight_ref, adj_ref, seed_ref, self_ref, own_ref, sems, out_sems,
):
    seed_blocks, tiles, side, _ = weight_ref.shape
    pairs = [(weight_hbm.at[b], weight_ref.at[b]) for b in range(seed_blocks)]
    pairs += [(seed_hbm, seed_ref), (self_hbm, self_ref), (table_hbm, table_ref)]
    loads = [pltpu.make_async_copy(src, dst, sems.at[i]) for i, (src, dst) in enumerate(pairs)]
    for load in loads:
        load.start()
    slots = adj_ref.shape[1] // live_ref.shape[1]
    lane = lax.broadcasted_iota(jnp.int32, (side, side), 1)
    stores = []
    for b in range(seed_blocks):
        loads[b].wait()
        lines = slice(b * side, (b + 1) * side)
        for k in range(tiles):
            block = block_ref[b, k]
            limit = jnp.where(lane < slots, live_ref[0, 2 * block], live_ref[0, 2 * block + 1] + slots)
            tile = jnp.where(lane < limit, weight_ref[b, k].astype(F32), 0.0)
            start = pl.multiple_of(block * side, side)
            adj_ref[lines, pl.ds(start, side)] = tile.astype(BF16)
        part = pl.ds(b * side, side)
        stores.append(pltpu.make_async_copy(adj_ref.at[part], adj_hbm.at[part], out_sems.at[b]))
        stores[b].start()
    for load in loads[seed_blocks:]:
        load.wait()
    for b in range(seed_blocks):
        part = pl.ds(b * side, side)
        own_ref[part, :] = jnp.dot(seed_ref[part, :], self_ref[...], preferred_element_type=F32) + bias_ref[...]
        stores.append(pltpu.make_async_copy(own_ref.at[part], own_hbm.at[part], out_sems.at[seed_blocks + b]))
        stores[seed_blocks + b].start()
    for store in stores:
        store.wait()


def stage(tile_block, live_count, tile_weight, table, seeds, self_weight, bias):
    seed_blocks, tiles, side, _ = tile_weight.shape
    targets, hidden = seeds.shape[0], self_weight.shape[1]
    near, far = pl.BlockSpec(memory_space=pltpu.VMEM), pl.BlockSpec(memory_space=pltpu.HBM)
    scalars = pl.BlockSpec(memory_space=pltpu.SMEM)
    shape = (seed_blocks * side, tiles * side)
    return pl.pallas_call(
        stage_kernel,
        out_shape=(pltpu.HBM(shape, BF16), pltpu.HBM((targets, hidden), F32), pltpu.VMEM(table.shape, BF16)),
        in_specs=[scalars, scalars, far, far, far, far, near],
        out_specs=(far, far, near),
        scratch_shapes=[
            pltpu.VMEM(tile_weight.shape, BF16),
            pltpu.VMEM(shape, BF16),
            pltpu.VMEM(seeds.shape, BF16),
            pltpu.VMEM(self_weight.shape, BF16),
            pltpu.VMEM((targets, hidden), F32),
            pltpu.SemaphoreType.DMA((seed_blocks + 3,)),
            pltpu.SemaphoreType.DMA((2 * seed_blocks,)),
        ],
        compiler_params=params(),
        cost_estimate=pl.CostEstimate(
            flops=2 * targets * seeds.shape[1] * hidden, bytes_accessed=7 * 10**6, transcendentals=0
        ),
        name="stage",
    )(
        in_hbm(tile_block),
        in_hbm(live_count.reshape(1, -1)),
        in_hbm(tile_weight),
        in_hbm(table),
        in_hbm(seeds),
        in_hbm(self_weight),
        in_hbm(bias.reshape(1, -1)),
    )


def pick_rows(asked, table):
    owners, _, slots = asked.shape
    rows, width = table.shape
    pieces = 8
    return pl.pallas_call(
        pick_kernel,
        out_shape=pltpu.HBM((owners * slots, width), BF16),
        in_specs=[pl.BlockSpec(memory_space=pltpu.VMEM), pl.BlockSpec(memory_space=pltpu.VMEM)],
        out_specs=pl.BlockSpec(memory_space=pltpu.HBM),
        scratch_shapes=[
            pltpu.VMEM((owners * slots, rows), BF16),
            pltpu.VMEM((owners * slots, width), BF16),
            pltpu.SemaphoreType.DMA((pieces,)),
        ],
        compiler_params=params(),
        cost_estimate=pl.CostEstimate(
            flops=2 * owners * slots * rows * width, bytes_accessed=5 * 10**6, transcendentals=0
        ),
        name="pick_rows",
    )(asked, in_vmem(table))


def turned(left, right):
    return lax.dot_general(left, right, (((0,), (0,)), ((), ())), preferred_element_type=F32)


def units_of(grad, core, span):
    hidden = grad.shape[1]
    unit = lax.broadcasted_iota(jnp.int32, (hidden, hidden // 2), 0)
    place = lax.broadcasted_iota(jnp.int32, (hidden, hidden // 2), 1)
    chosen = unit == place + (place // span + core) * span
    return jnp.dot(grad, jnp.where(chosen, 1.0, 0.0).astype(BF16), preferred_element_type=F32).astype(BF16)


def layer_kernel(
    span, core_ref, adj_ref, rows_ref, neigh_ref, own_hbm, cot_hbm, send_ref, grad_ref, agg_ref,
    own_ref, cot_ref, sems,
):
    pairs = [(own_hbm, own_ref), (cot_hbm, cot_ref)]
    loads = [pltpu.make_async_copy(src, dst, sems.at[i]) for i, (src, dst) in enumerate(pairs)]
    for load in loads:
        load.start()
    agg_ref[...] = jnp.dot(adj_ref[...], rows_ref[...], preferred_element_type=F32).astype(BF16)
    for load in loads:
        load.wait()
    targets = grad_ref.shape[0]
    step = targets // 4
    for start in range(0, targets, step):
        part = slice(start, start + step)
        pre = own_ref[part, :] + jnp.dot(agg_ref[part, :], neigh_ref[...], preferred_element_type=F32)
        s = 1.0 / (1.0 + jnp.exp(-pre))
        slope = s * (1.0 + pre * (1.0 - s))
        grad_ref[part, :] = (cot_ref[part, :].astype(F32) * slope).astype(BF16)
    other = units_of(grad_ref[...], 1 - core_ref[0], span)
    send_ref[...] = turned(other, agg_ref[...]).astype(BF16)


def layer(core, adj, rows, neigh, own, cot, span):
    targets, fetched = adj.shape
    width, hidden = neigh.shape
    near, far = pl.BlockSpec(memory_space=pltpu.VMEM), pl.BlockSpec(memory_space=pltpu.HBM)
    return pl.pallas_call(
        functools.partial(layer_kernel, span),
        out_shape=(
            pltpu.VMEM((hidden // 2, width), BF16),
            pltpu.VMEM((targets, hidden), BF16),
            pltpu.VMEM((targets, width), BF16),
        ),
        in_specs=[pl.BlockSpec(memory_space=pltpu.SMEM), near, near, near, far, far],
        out_specs=(near, near, near),
        scratch_shapes=[
            pltpu.VMEM((targets, hidden), F32),
            pltpu.VMEM((targets, hidden), BF16),
            pltpu.SemaphoreType.DMA((2,)),
        ],
        compiler_params=params(),
        cost_estimate=pl.CostEstimate(
            flops=2 * targets * width * (fetched + 2 * hidden),
            bytes_accessed=8 * 10**6,
            transcendentals=targets * hidden,
        ),
        name="layer",
    )(core, adj, rows, neigh, in_hbm(own), in_hbm(cot))


def own_term_kernel(span, core_ref, grad_ref, agg_ref, keep_ref):
    keep_ref[...] = turned(units_of(grad_ref[...], core_ref[0], span), agg_ref[...])


def own_term(core, grad, agg, span):
    targets, hidden = grad.shape
    width = agg.shape[1]
    near = pl.BlockSpec(memory_space=pltpu.VMEM)
    return pl.pallas_call(
        functools.partial(own_term_kernel, span),
        out_shape=pltpu.VMEM((hidden // 2, width), F32),
        in_specs=[pl.BlockSpec(memory_space=pltpu.SMEM), near, near],
        out_specs=near,
        compiler_params=params(),
        cost_estimate=pl.CostEstimate(
            flops=2 * targets * (width + hidden) * (hidden // 2), bytes_accessed=2 * 10**6, transcendentals=0
        ),
        name="own_term",
    )(core, grad, agg)


def body(
    features,
    fetch_row,
    live_count,
    seed_features,
    tile_block,
    tile_weight,
    self_weight,
    neighbour_weight,
    layer_bias,
    cotangent,
):
    owners, slots = fetch_row.shape
    width, hidden = neighbour_weight.shape
    nx, nc, nz, ny = (lax.axis_size(a) for a in EVERY)
    span = hidden // (nx * nc)
    asked = lax.all_to_all(fetch_row.reshape(owners, 1, slots), GRP, split_axis=0, concat_axis=0, tiled=True)
    adj, own, table = stage(
        tile_block, live_count, tile_weight, features, seed_features, self_weight, layer_bias
    )
    picked = pick_rows(asked, table)
    rows = lax.all_to_all(picked.reshape(owners, slots, width), GRP, split_axis=0, concat_axis=0, tiled=True)
    core = lax.axis_index("c").astype(jnp.int32).reshape(1)
    send, grad, agg = layer(
        core, adj, rows.reshape(owners * slots, width), neighbour_weight, own, cotangent, span
    )
    got = lax.ppermute(send, "c", [(0, 1), (1, 0)])
    keep = own_term(core, grad, agg, span)
    pair = (keep + got.astype(F32)).astype(BF16).reshape(nx, span, width)
    parts = lax.all_to_all(pair, "x", split_axis=0, concat_axis=0, tiled=True)
    ring = jnp.sum(parts.astype(F32), axis=0)
    cols = width // (nz * ny)
    pieces = ring.reshape(span, nz * ny, cols).transpose(1, 2, 0).reshape(nz * ny, cols * span)
    pieces = lax.all_to_all(pieces, REP, split_axis=0, concat_axis=0, tiled=True)
    return jnp.sum(pieces, axis=0).reshape(cols, span).T


def solution(mesh):
    n_grp, n_rep = mesh.shape["grp"], mesh.shape["rep"]
    chips, lines = n_grp // 2, int(round(n_rep**0.5))
    fine = Mesh(mesh.devices.reshape(chips, 2, lines, n_rep // lines), EVERY)
    placed = (
        P(EVERY, None),
        P(GRP, REP),
        P(GRP, REP),
        P(EVERY, None),
        P(EVERY, None),
        P(EVERY, None, None, None),
        P(),
        P(),
        P(),
        P(EVERY, None),
    )
    return jax.shard_map(body, mesh=fine, in_specs=placed, out_specs=P(GRP, REP), check_vma=False)
```

time: 122 us -> 121 us (level)
  waiting for transfers between devices: 37.5 us -> 41.8 us
  local copies, waits for them, and re-layouts: 4.63 us -> 1.22 us
  Pallas kernels: 11.4 us -> 9.5 us
    all_to_all x1, waiting for transfers between devices: 30.2 us -> 37.9 us  [body(): lax.all_to_all(picked.reshape(owners, slots, width), GRP, split_axis=0, c...]
    unnamed x17 -> x4, local copies, waits for them, and re-layouts: 3.42 us -> 0.01 us
    all_to_all x1, waiting for transfers between devices: 6.35 us -> 3.44 us  [body(): lax.all_to_all(fetch_row.reshape(owners, 1, slots), GRP, split_axis=0, co...]
    pallas_call x4 -> x3, Pallas kernels: 9.56 us -> 7.65 us  [the longest x1 4.05 us: stage(): pl.pallas_call(stage_kernel, out_shape=(pltpu.HBM(shape, BF16), pltpu.HBM...]
  transfers between devices with their start and end apart: 3 -> 3, of which waited for: 3 -> 3; matrix products, arithmetic and copies ran while one was open for 0% -> 0% of each run, Pallas kernels for 5% -> 4%
where the time goes in v5:
time: 121 us; the launch traced here: 120 us
  blocking collectives  53.7 us (44%)
  waiting for transfers between devices  41.8 us (35%)
  starting transfers between devices  13.7 us (11%)
  Pallas kernels  9.5 us (8%)
  local copies, waits for them, and re-layouts  1.22 us (1%)
    all_to_all x1, waiting for transfers between devices, body(): lax.all_to_all(picked.reshape(owners, slots, width), GRP, split_axis=0, c...  37.9 us
    all_to_all x1, blocking collectives, body(): lax.all_to_all(pieces, REP, split_axis=0, concat_axis=0, tiled=True)  34.8 us
    all_to_all x1, blocking collectives, body(): parts = lax.all_to_all(pair, 'x', split_axis=0, concat_axis=0, tiled=True)  18.9 us
    all_to_all x1, starting transfers between devices, body(): lax.all_to_all(fetch_row.reshape(owners, 1, slots), GRP, split_axis=0, co...  6.86 us
    pallas_call x1, Pallas kernels, stage(): pl.pallas_call(stage_kernel, out_shape=(pltpu.HBM(shape, BF16), pltpu.HBM...  4.05 us
    all_to_all x1, starting transfers between devices, body(): lax.all_to_all(picked.reshape(owners, slots, width), GRP, split_axis=0, c...  3.92 us
    all_to_all x1, waiting for transfers between devices, body(): lax.all_to_all(fetch_row.reshape(owners, 1, slots), GRP, split_axis=0, co...  3.44 us
    ppermute x1, starting transfers between devices, body(): got = lax.ppermute(send, 'c', [(0, 1), (1, 0)])  2.89 us
  transfers between devices with their start and end apart: 3, of which 3 were waited for; matrix products, arithmetic and copies ran while one was open for 0% of the time, Pallas kernels for 4%

profile of v5, /device:TPU:16, one launch (start us, length us, event | category | flops | bytes accessed | tf_op | source)
XLA Modules:
  0.0 120.2 jit_solution(17055233634965502676)
XLA Ops:
  0.0 6.9 %all-to-all-start = ((s32[16,1,64]{2,1,0:T(1,128)}), s32[16,1,64]{2,1,0:T(1,128)S(1)}, u32[]{:S(2)}, u32[]{:S(2)}) async-start(s32[16,1,64]{2,1,0:T(1,128)} %bitcast.17), calls=%async_computation | async-start | bytes 16384 | tf_op jit(solution)/shard_map/all_to_all | solution.py:252
  6.9 4.1 %stage.1 = (bf16[512,1024]{1,0:T(8,128)(2,1)}, f32[512,512]{1,0:T(8,128)}, bf16[512,768]{1,0:T(8,128)(2,1)S(1)}) custom-call(s32[4,8]{1,0:T(4,128)} %block_ref.1, s32[1,16]{1,0:T(1,128)} %bitcast.19, bf16[4,8,128,128]{3,2,1,0:T(8,128)(2,1)} %weight_hbm.1, bf16[512,768]{1,0:T(8,128)(2,1)} %table_hbm.1, bf16[512,768]{1,0:T(8,128)(2,1)} %seed_hbm.1, ...), custom_call_target="tpu_custom_call" | custom-call | flops 402653184 | bytes 7000000 | tf_op jit(solution)/shard_map/stage/pallas_call | solution.py:100
  10.9 3.4 %all-to-all-done.asked_ref = s32[16,1,64]{2,1,0:T(1,128)S(1)} async-done(((s32[16,1,64]{2,1,0:T(1,128)}), s32[16,1,64]{2,1,0:T(1,128)S(1)}, u32[]{:S(2)}, u32[]{:S(2)}) %all-to-all-start) | async-done | bytes 4128 | tf_op jit(solution)/shard_map/all_to_all | solution.py:252
  14.4 1.8 %pick_rows.1 = bf16[1024,768]{1,0:T(8,128)(2,1)} custom-call(s32[16,1,64]{2,1,0:T(1,128)S(1)} %all-to-all-done.asked_ref, bf16[512,768]{1,0:T(8,128)(2,1)S(1)} %get-tuple-element.12.table_ref), custom_call_target="tpu_custom_call" | custom-call | flops 805306368 | bytes 5000000 | tf_op jit(solution)/shard_map/pick_rows/pallas_call | solution.py:134
  16.2 0.0 copy-start
  16.2 0.0 copy-start.1
  16.2 3.9 %all-to-all-start.1 = ((bf16[16,64,768]{2,1,0:T(8,128)(2,1)}), bf16[16,64,768]{2,1,0:T(8,128)(2,1)S(1)}, u32[]{:S(2)}, u32[]{:S(2)}) async-start(bf16[16,64,768]{2,1,0:T(8,128)(2,1)} %bitcast.14), calls=%async_computation.1 | async-start | bytes 3145728 | tf_op jit(solution)/shard_map/all_to_all | solution.py:257
  20.2 37.9 %all-to-all-done.1 = bf16[16,64,768]{2,1,0:T(8,128)(2,1)S(1)} async-done(((bf16[16,64,768]{2,1,0:T(8,128)(2,1)}), bf16[16,64,768]{2,1,0:T(8,128)(2,1)S(1)}, u32[]{:S(2)}, u32[]{:S(2)}) %all-to-all-start.1) | async-done | bytes 1572896 | tf_op jit(solution)/shard_map/all_to_all | solution.py:257
  58.0 0.0 copy-done
  58.0 0.0 copy-done.1
  58.0 2.8 %layer.1 = (bf16[256,768]{1,0:T(8,128)(2,1)S(1)}, bf16[512,512]{1,0:T(8,128)(2,1)S(1)}, bf16[512,768]{1,0:T(8,128)(2,1)S(1)}) custom-call(s32[1]{0:T(128)} %bitcast.core_ref, bf16[512,1024]{1,0:T(8,128)(2,1)S(1)} %copy-done, bf16[1024,768]{1,0:T(8,128)(2,1)S(1)} %bitcast.12, bf16[768,512]{1,0:T(8,128)(2,1)S(1)} %copy-done.1, ...), custom_call_target="tpu_custom_call" | custom-call | flops 1610612736 | bytes 8000000 | tf_op jit(solution)/shard_map/layer/pallas_call | solution.py:191
  60.9 2.9 %collective-permute-start = (bf16[256,768]{1,0:T(8,128)(2,1)S(1)}, bf16[256,768]{1,0:T(8,128)(2,1)S(1)}, u32[]{:S(2)}, u32[]{:S(2)}) collective-permute-start(bf16[256,768]{1,0:T(8,128)(2,1)S(1)} %get-tuple-element.16), channel_id=1, source_target_pairs={{0,64},{64,0},{1,65},{65,1},{2,66},{66,2},{3,67},{67,3},{4,68},{68... | collective-permute-start | bytes 1179656 | tf_op jit(solution)/shard_map/ppermute | solution.py:262
  63.8 0.8 own_term.1
  64.6 0.6 collective-permute-done
  65.1 0.1 add_convert_fusion
  65.2 18.9 %all_to_all.24 = bf16[8,32,768]{2,1,0:T(8,128)(2,1)S(1)} all-to-all(bf16[8,32,768]{2,1,0:T(8,128)(2,1)S(1)} %bitcast.15), channel_id=1, replica_groups=mesh['x'=8,'c'=2,'z'=8,'y'=8] {'x'}, dimensions={0} | all-to-all | bytes 786432 | tf_op jit(solution)/shard_map/all_to_all | solution.py:265
  84.1 0.1 convert_reduce_fusion
  84.1 0.2 copy.12
  84.3 0.2 copy.13
  84.5 0.1 copy.14
  84.7 34.8 %all_to_all.25 = f32[64,1,384]{2,1,0:T(1,128)S(1)} all-to-all(f32[64,1,384]{2,1,0:T(1,128)S(1)} %copy.14), channel_id=1, replica_groups=mesh['x'=8,'c'=2,'z'=8,'y'=8] {'z','y'}, dimensions={0} | all-to-all | bytes 196608 | tf_op jit(solution)/shard_map/all_to_all | solution.py:269
  119.5 0.1 reduce_sum.19
  119.6 0.7 reshape.39
  (1 shorter events, 0.0 us)
Async XLA Ops:
  0.0 14.4 %all-to-all-start = ((s32[16,1,64]{2,1,0:T(1,128)}), s32[16,1,64]{2,1,0:T(1,128)S(1)}, u32[]{:S(2)}, u32[]{:S(2)}) async-start(s32[16,1,64]{2,1,0:T(1,128)} %bitcast.17), calls=%async_computation | async-start | bytes 16384 | tf_op jit(solution)/shard_map/all_to_all | solution.py:252
  16.2 41.8 %copy-start = (bf16[512,1024]{1,0:T(8,128)(2,1)S(1)}, bf16[512,1024]{1,0:T(8,128)(2,1)}, u32[]{:S(2)}) copy-start(bf16[512,1024]{1,0:T(8,128)(2,1)} %get-tuple-element.11.adj_ref) | copy-start | bytes 3145732
  16.2 41.8 %copy-start.1 = (bf16[768,512]{1,0:T(8,128)(2,1)S(1)}, bf16[768,512]{1,0:T(8,128)(2,1)}, u32[]{:S(2)}) copy-start(bf16[768,512]{1,0:T(8,128)(2,1)} %neigh_ref.1) | copy-start | bytes 2359300
  16.2 41.8 %all-to-all-start.1 = ((bf16[16,64,768]{2,1,0:T(8,128)(2,1)}), bf16[16,64,768]{2,1,0:T(8,128)(2,1)S(1)}, u32[]{:S(2)}, u32[]{:S(2)}) async-start(bf16[16,64,768]{2,1,0:T(8,128)(2,1)} %bitcast.14), calls=%async_computation.1 | async-start | bytes 3145728 | tf_op jit(solution)/shard_map/all_to_all | solution.py:257
  60.9 4.2 %collective-permute-start = (bf16[256,768]{1,0:T(8,128)(2,1)S(1)}, bf16[256,768]{1,0:T(8,128)(2,1)S(1)}, u32[]{:S(2)}, u32[]{:S(2)}) collective-permute-start(bf16[256,768]{1,0:T(8,128)(2,1)S(1)} %get-tuple-element.16), channel_id=1, source_target_pairs={{0,64},{64,0},{1,65},{65,1},{2,66},{66,2},{3,67},{67,3},{4,68},{68... | collective-permute-start | bytes 1179656 | tf_op jit(solution)/shard_map/ppermute | solution.py:262

commit v6 on v5

--- a/solution.py
+++ b/solution.py
@@ -2,6 +2,7 @@
 
 import jax
 import jax.numpy as jnp
+import numpy as np
 from jax import lax
 from jax.experimental import pallas as pl
 from jax.experimental.pallas import tpu as pltpu
@@ -233,6 +234,46 @@
     )(core, grad, agg)
 
 
+def pair_kernel(core_ref, keep_ref, got_ref, pair_ref):
+    blocks, span, width = pair_ref.shape
+    cut = width // blocks
+    total = (keep_ref[...] + got_ref[...].astype(F32)).astype(BF16)
+
+    @pl.when(core_ref[0] == 0)
+    def _():
+        for x in range(blocks):
+            pair_ref[x] = total[x * span : (x + 1) * span, :]
+
+    @pl.when(core_ref[0] == 1)
+    def _():
+        for z in range(blocks):
+            parts = [total[x * span : (x + 1) * span, z * cut : (z + 1) * cut] for x in range(blocks)]
+            pair_ref[z] = jnp.concatenate(parts, axis=1)
+
+
+def pair_sum(core, keep, got, blocks):
+    rows, width = keep.shape
+    near = pl.BlockSpec(memory_space=pltpu.VMEM)
+    return pl.pallas_call(
+        pair_kernel,
+        out_shape=pltpu.VMEM((blocks, rows // blocks, width), BF16),
+        in_specs=[pl.BlockSpec(memory_space=pltpu.SMEM), near, near],
+        out_specs=near,
+        compiler_params=params(),
+        name="pair_sum",
+    )(core, keep, got)
+
+
+def by_core(sizes, first, second):
+    ranks = np.arange(np.prod(sizes)).reshape(sizes)
+    groups = []
+    for core, axes in enumerate((first, second)):
+        rest = [a for a in (0, 2, 3) if a not in axes]
+        half = np.expand_dims(ranks[:, core], 1).transpose(*rest, 1, *axes)
+        groups += half.reshape(-1, int(np.prod([sizes[a] for a in axes]))).tolist()
+    return groups
+
+
 def body(
     features,
     fetch_row,
@@ -261,12 +302,17 @@
     )
     got = lax.ppermute(send, "c", [(0, 1), (1, 0)])
     keep = own_term(core, grad, agg, span)
-    pair = (keep + got.astype(F32)).astype(BF16).reshape(nx, span, width)
-    parts = lax.all_to_all(pair, "x", split_axis=0, concat_axis=0, tiled=True)
+    sizes = (nx, nc, nz, ny)
+    pair = pair_sum(core, keep, got, nx)
+    parts = lax.all_to_all(
+        pair, EVERY, split_axis=0, concat_axis=0, tiled=True, axis_index_groups=by_core(sizes, (0,), (2,))
+    )
     ring = jnp.sum(parts.astype(F32), axis=0)
     cols = width // (nz * ny)
     pieces = ring.reshape(span, nz * ny, cols).transpose(1, 2, 0).reshape(nz * ny, cols * span)
-    pieces = lax.all_to_all(pieces, REP, split_axis=0, concat_axis=0, tiled=True)
+    pieces = lax.all_to_all(
+        pieces, EVERY, split_axis=0, concat_axis=0, tiled=True, axis_index_groups=by_core(sizes, (2, 3), (0, 3))
+    )
     return jnp.sum(pieces, axis=0).reshape(cols, span).T
 
 

time: 121 us -> 118 us (0.975)
  blocking collectives: 53.7 us -> 50.6 us
    all_to_all x2, blocking collectives: 53.7 us -> 50.6 us  [the longest x1 34.8 us: body(): lax.all_to_all(pieces, EVERY, split_axis=0, concat_axis=0, tiled=True, ax...]
where the time goes in v6:
time: 118 us; the launch traced here: 117 us
  blocking collectives  50.6 us (43%)
  waiting for transfers between devices  41.9 us (36%)
  starting transfers between devices  13.7 us (12%)
  Pallas kernels  9.65 us (8%)
  local copies, waits for them, and re-layouts  1.22 us (1%)
    all_to_all x1, waiting for transfers between devices, body(): lax.all_to_all(picked.reshape(owners, slots, width), GRP, split_axis=0, c...  37.9 us
    all_to_all x1, blocking collectives, body(): lax.all_to_all(pieces, EVERY, split_axis=0, concat_axis=0, tiled=True, ax...  34.8 us
    all_to_all x1, blocking collectives, body(): lax.all_to_all(pair, EVERY, split_axis=0, concat_axis=0, tiled=True, axis...  15.8 us
    all_to_all x1, starting transfers between devices, body(): lax.all_to_all(fetch_row.reshape(owners, 1, slots), GRP, split_axis=0, co...  6.86 us
    pallas_call x1, Pallas kernels, stage(): pl.pallas_call(stage_kernel, out_shape=(pltpu.HBM(shape, BF16), pltpu.HBM...  4.05 us
    all_to_all x1, starting transfers between devices, body(): lax.all_to_all(picked.reshape(owners, slots, width), GRP, split_axis=0, c...  3.92 us
    all_to_all x1, waiting for transfers between devices, body(): lax.all_to_all(fetch_row.reshape(owners, 1, slots), GRP, split_axis=0, co...  3.44 us
    ppermute x1, starting transfers between devices, body(): got = lax.ppermute(send, 'c', [(0, 1), (1, 0)])  2.89 us
  transfers between devices with their start and end apart: 3, of which 3 were waited for; matrix products, arithmetic and copies ran while one was open for 0% of the time, Pallas kernels for 4%

profile of v6, /device:TPU:16, one launch (start us, length us, event | category | flops | bytes accessed | tf_op | source)
XLA Modules:
  0.0 117.2 jit_solution(4629189274686951914)
XLA Ops:
  0.0 6.9 %all-to-all-start = ((s32[16,1,64]{2,1,0:T(1,128)}), s32[16,1,64]{2,1,0:T(1,128)S(1)}, u32[]{:S(2)}, u32[]{:S(2)}) async-start(s32[16,1,64]{2,1,0:T(1,128)} %bitcast.15), calls=%async_computation | async-start | bytes 16384 | tf_op jit(solution)/shard_map/all_to_all | solution.py:293
  6.9 4.1 %stage.1 = (bf16[512,1024]{1,0:T(8,128)(2,1)}, f32[512,512]{1,0:T(8,128)}, bf16[512,768]{1,0:T(8,128)(2,1)S(1)}) custom-call(s32[4,8]{1,0:T(4,128)} %block_ref.1, s32[1,16]{1,0:T(1,128)} %bitcast.17, bf16[4,8,128,128]{3,2,1,0:T(8,128)(2,1)} %weight_hbm.1, bf16[512,768]{1,0:T(8,128)(2,1)} %table_hbm.1, bf16[512,768]{1,0:T(8,128)(2,1)} %seed_hbm.1, ...), custom_call_target="tpu_custom_call" | custom-call | flops 402653184 | bytes 7000000 | tf_op jit(solution)/shard_map/stage/pallas_call | solution.py:101
  10.9 3.4 %all-to-all-done.asked_ref = s32[16,1,64]{2,1,0:T(1,128)S(1)} async-done(((s32[16,1,64]{2,1,0:T(1,128)}), s32[16,1,64]{2,1,0:T(1,128)S(1)}, u32[]{:S(2)}, u32[]{:S(2)}) %all-to-all-start) | async-done | bytes 4128 | tf_op jit(solution)/shard_map/all_to_all | solution.py:293
  14.4 1.8 %pick_rows.1 = bf16[1024,768]{1,0:T(8,128)(2,1)} custom-call(s32[16,1,64]{2,1,0:T(1,128)S(1)} %all-to-all-done.asked_ref, bf16[512,768]{1,0:T(8,128)(2,1)S(1)} %get-tuple-element.12.table_ref), custom_call_target="tpu_custom_call" | custom-call | flops 805306368 | bytes 5000000 | tf_op jit(solution)/shard_map/pick_rows/pallas_call | solution.py:135
  16.2 0.0 copy-start
  16.2 0.0 copy-start.1
  16.2 3.9 %all-to-all-start.1 = ((bf16[16,64,768]{2,1,0:T(8,128)(2,1)}), bf16[16,64,768]{2,1,0:T(8,128)(2,1)S(1)}, u32[]{:S(2)}, u32[]{:S(2)}) async-start(bf16[16,64,768]{2,1,0:T(8,128)(2,1)} %bitcast.13), calls=%async_computation.1 | async-start | bytes 3145728 | tf_op jit(solution)/shard_map/all_to_all | solution.py:298
  20.2 37.9 %all-to-all-done.1 = bf16[16,64,768]{2,1,0:T(8,128)(2,1)S(1)} async-done(((bf16[16,64,768]{2,1,0:T(8,128)(2,1)}), bf16[16,64,768]{2,1,0:T(8,128)(2,1)S(1)}, u32[]{:S(2)}, u32[]{:S(2)}) %all-to-all-start.1) | async-done | bytes 1572896 | tf_op jit(solution)/shard_map/all_to_all | solution.py:298
  58.0 0.0 copy-done
  58.0 0.0 copy-done.1
  58.0 2.8 %layer.1 = (bf16[256,768]{1,0:T(8,128)(2,1)S(1)}, bf16[512,512]{1,0:T(8,128)(2,1)S(1)}, bf16[512,768]{1,0:T(8,128)(2,1)S(1)}) custom-call(s32[1]{0:T(128)} %bitcast.core_ref, bf16[512,1024]{1,0:T(8,128)(2,1)S(1)} %copy-done, bf16[1024,768]{1,0:T(8,128)(2,1)S(1)} %bitcast.11, bf16[768,512]{1,0:T(8,128)(2,1)S(1)} %copy-done.1, ...), custom_call_target="tpu_custom_call" | custom-call | flops 1610612736 | bytes 8000000 | tf_op jit(solution)/shard_map/layer/pallas_call | solution.py:192
  60.9 2.9 %collective-permute-start = (bf16[256,768]{1,0:T(8,128)(2,1)S(1)}, bf16[256,768]{1,0:T(8,128)(2,1)S(1)}, u32[]{:S(2)}, u32[]{:S(2)}) collective-permute-start(bf16[256,768]{1,0:T(8,128)(2,1)S(1)} %get-tuple-element.16), channel_id=1, source_target_pairs={{0,64},{64,0},{1,65},{65,1},{2,66},{66,2},{3,67},{67,3},{4,68},{68... | collective-permute-start | bytes 1179656 | tf_op jit(solution)/shard_map/ppermute | solution.py:303
  63.8 0.8 own_term.1.keep_ref
  64.5 0.6 collective-permute-done.got_ref
  65.1 0.2 pair_sum.1
  65.3 15.8 %all_to_all.24 = bf16[8,32,768]{2,1,0:T(8,128)(2,1)S(1)} all-to-all(bf16[8,32,768]{2,1,0:T(8,128)(2,1)S(1)} %pair_sum.1), channel_id=1, replica_groups={{0,128,256,384,512,640,768,896},{1,129,257,385,513,641,769,897},{2,130,..., dimensions={0} | all-to-all | bytes 786432 | tf_op jit(solution)/shard_map/all_to_all | solution.py:307
  81.1 0.1 convert_reduce_fusion
  81.1 0.2 copy.12
  81.3 0.2 copy.13
  81.5 0.1 copy.14
  81.7 34.8 %all_to_all.25 = f32[64,1,384]{2,1,0:T(1,128)S(1)} all-to-all(f32[64,1,384]{2,1,0:T(1,128)S(1)} %copy.14), channel_id=1, replica_groups={{0,1,2,3,4,5,6,7,8,9,10,11,12,13,14,15,16,17,18,19,20,21,22,23,24,25,26..., dimensions={0} | all-to-all | bytes 196608 | tf_op jit(solution)/shard_map/all_to_all | solution.py:313
  116.5 0.1 reduce_sum.19
  116.6 0.7 reshape.35
  (1 shorter events, 0.0 us)
Async XLA Ops:
  0.0 14.4 %all-to-all-start = ((s32[16,1,64]{2,1,0:T(1,128)}), s32[16,1,64]{2,1,0:T(1,128)S(1)}, u32[]{:S(2)}, u32[]{:S(2)}) async-start(s32[16,1,64]{2,1,0:T(1,128)} %bitcast.15), calls=%async_computation | async-start | bytes 16384 | tf_op jit(solution)/shard_map/all_to_all | solution.py:293
  16.2 41.8 %copy-start = (bf16[512,1024]{1,0:T(8,128)(2,1)S(1)}, bf16[512,1024]{1,0:T(8,128)(2,1)}, u32[]{:S(2)}) copy-start(bf16[512,1024]{1,0:T(8,128)(2,1)} %get-tuple-element.11.adj_ref) | copy-start | bytes 3145732
  16.2 41.8 %copy-start.1 = (bf16[768,512]{1,0:T(8,128)(2,1)S(1)}, bf16[768,512]{1,0:T(8,128)(2,1)}, u32[]{:S(2)}) copy-start(bf16[768,512]{1,0:T(8,128)(2,1)} %neigh_ref.1) | copy-start | bytes 2359300
  16.2 41.8 %all-to-all-start.1 = ((bf16[16,64,768]{2,1,0:T(8,128)(2,1)}), bf16[16,64,768]{2,1,0:T(8,128)(2,1)S(1)}, u32[]{:S(2)}, u32[]{:S(2)}) async-start(bf16[16,64,768]{2,1,0:T(8,128)(2,1)} %bitcast.13), calls=%async_computation.1 | async-start | bytes 3145728 | tf_op jit(solution)/shard_map/all_to_all | solution.py:298
  60.9 4.2 %collective-permute-start = (bf16[256,768]{1,0:T(8,128)(2,1)S(1)}, bf16[256,768]{1,0:T(8,128)(2,1)S(1)}, u32[]{:S(2)}, u32[]{:S(2)}) collective-permute-start(bf16[256,768]{1,0:T(8,128)(2,1)S(1)} %get-tuple-element.16), channel_id=1, source_target_pairs={{0,64},{64,0},{1,65},{65,1},{2,66},{66,2},{3,67},{67,3},{4,68},{68... | collective-permute-start | bytes 1179656 | tf_op jit(solution)/shard_map/ppermute | solution.py:303

commit v7 on v6

--- a/solution.py
+++ b/solution.py
@@ -178,7 +178,7 @@
     for start in range(0, targets, step):
         part = slice(start, start + step)
         pre = own_ref[part, :] + jnp.dot(agg_ref[part, :], neigh_ref[...], preferred_element_type=F32)
-        s = 1.0 / (1.0 + jnp.exp(-pre))
+        s = 0.5 * jnp.tanh(0.5 * pre) + 0.5
         slope = s * (1.0 + pre * (1.0 - s))
         grad_ref[part, :] = (cot_ref[part, :].astype(F32) * slope).astype(BF16)
     other = units_of(grad_ref[...], 1 - core_ref[0], span)

time: 118 us -> 118 us (level)
  no operation moved by 1% of the time
where the time goes in v7:
time: 118 us; the launch traced here: 117 us
  blocking collectives  50.6 us (43%)
  waiting for transfers between devices  41.8 us (35%)
  starting transfers between devices  13.7 us (12%)
  Pallas kernels  9.64 us (8%)
  local copies, waits for them, and re-layouts  1.22 us (1%)
    all_to_all x1, waiting for transfers between devices, body(): lax.all_to_all(picked.reshape(owners, slots, width), GRP, split_axis=0, c...  37.9 us
    all_to_all x1, blocking collectives, body(): lax.all_to_all(pieces, EVERY, split_axis=0, concat_axis=0, tiled=True, ax...  34.8 us
    all_to_all x1, blocking collectives, body(): lax.all_to_all(pair, EVERY, split_axis=0, concat_axis=0, tiled=True, axis...  15.8 us
    all_to_all x1, starting transfers between devices, body(): lax.all_to_all(fetch_row.reshape(owners, 1, slots), GRP, split_axis=0, co...  6.86 us
    pallas_call x1, Pallas kernels, stage(): pl.pallas_call(stage_kernel, out_shape=(pltpu.HBM(shape, BF16), pltpu.HBM...  4.05 us
    all_to_all x1, starting transfers between devices, body(): lax.all_to_all(picked.reshape(owners, slots, width), GRP, split_axis=0, c...  3.92 us
    all_to_all x1, waiting for transfers between devices, body(): lax.all_to_all(fetch_row.reshape(owners, 1, slots), GRP, split_axis=0, co...  3.44 us
    ppermute x1, starting transfers between devices, body(): got = lax.ppermute(send, 'c', [(0, 1), (1, 0)])  2.9 us
  transfers between devices with their start and end apart: 3, of which 3 were waited for; matrix products, arithmetic and copies ran while one was open for 0% of the time, Pallas kernels for 4%

profile of v7, /device:TPU:16, one launch (start us, length us, event | category | flops | bytes accessed | tf_op | source)
XLA Modules:
  0.0 117.2 jit_solution(15909483821926926255)
XLA Ops:
  0.0 6.9 %all-to-all-start = ((s32[16,1,64]{2,1,0:T(1,128)}), s32[16,1,64]{2,1,0:T(1,128)S(1)}, u32[]{:S(2)}, u32[]{:S(2)}) async-start(s32[16,1,64]{2,1,0:T(1,128)} %bitcast.15), calls=%async_computation | async-start | bytes 16384 | tf_op jit(solution)/shard_map/all_to_all | solution.py:293
  6.9 4.1 %stage.1 = (bf16[512,1024]{1,0:T(8,128)(2,1)}, f32[512,512]{1,0:T(8,128)}, bf16[512,768]{1,0:T(8,128)(2,1)S(1)}) custom-call(s32[4,8]{1,0:T(4,128)} %block_ref.1, s32[1,16]{1,0:T(1,128)} %bitcast.17, bf16[4,8,128,128]{3,2,1,0:T(8,128)(2,1)} %weight_hbm.1, bf16[512,768]{1,0:T(8,128)(2,1)} %table_hbm.1, bf16[512,768]{1,0:T(8,128)(2,1)} %seed_hbm.1, ...), custom_call_target="tpu_custom_call" | custom-call | flops 402653184 | bytes 7000000 | tf_op jit(solution)/shard_map/stage/pallas_call | solution.py:101
  10.9 3.4 %all-to-all-done.asked_ref = s32[16,1,64]{2,1,0:T(1,128)S(1)} async-done(((s32[16,1,64]{2,1,0:T(1,128)}), s32[16,1,64]{2,1,0:T(1,128)S(1)}, u32[]{:S(2)}, u32[]{:S(2)}) %all-to-all-start) | async-done | bytes 4128 | tf_op jit(solution)/shard_map/all_to_all | solution.py:293
  14.4 1.8 %pick_rows.1 = bf16[1024,768]{1,0:T(8,128)(2,1)} custom-call(s32[16,1,64]{2,1,0:T(1,128)S(1)} %all-to-all-done.asked_ref, bf16[512,768]{1,0:T(8,128)(2,1)S(1)} %get-tuple-element.12.table_ref), custom_call_target="tpu_custom_call" | custom-call | flops 805306368 | bytes 5000000 | tf_op jit(solution)/shard_map/pick_rows/pallas_call | solution.py:135
  16.2 0.0 copy-start
  16.2 0.0 copy-start.1
  16.2 3.9 %all-to-all-start.1 = ((bf16[16,64,768]{2,1,0:T(8,128)(2,1)}), bf16[16,64,768]{2,1,0:T(8,128)(2,1)S(1)}, u32[]{:S(2)}, u32[]{:S(2)}) async-start(bf16[16,64,768]{2,1,0:T(8,128)(2,1)} %bitcast.13), calls=%async_computation.1 | async-start | bytes 3145728 | tf_op jit(solution)/shard_map/all_to_all | solution.py:298
  20.2 37.9 %all-to-all-done.1 = bf16[16,64,768]{2,1,0:T(8,128)(2,1)S(1)} async-done(((bf16[16,64,768]{2,1,0:T(8,128)(2,1)}), bf16[16,64,768]{2,1,0:T(8,128)(2,1)S(1)}, u32[]{:S(2)}, u32[]{:S(2)}) %all-to-all-start.1) | async-done | bytes 1572896 | tf_op jit(solution)/shard_map/all_to_all | solution.py:298
  58.0 0.0 copy-done
  58.0 0.0 copy-done.1
  58.0 2.8 %layer.1 = (bf16[256,768]{1,0:T(8,128)(2,1)S(1)}, bf16[512,512]{1,0:T(8,128)(2,1)S(1)}, bf16[512,768]{1,0:T(8,128)(2,1)S(1)}) custom-call(s32[1]{0:T(128)} %bitcast.core_ref, bf16[512,1024]{1,0:T(8,128)(2,1)S(1)} %copy-done, bf16[1024,768]{1,0:T(8,128)(2,1)S(1)} %bitcast.11, bf16[768,512]{1,0:T(8,128)(2,1)S(1)} %copy-done.1, ...), custom_call_target="tpu_custom_call" | custom-call | flops 1610612736 | bytes 8000000 | tf_op jit(solution)/shard_map/layer/pallas_call | solution.py:192
  60.9 2.9 %collective-permute-start = (bf16[256,768]{1,0:T(8,128)(2,1)S(1)}, bf16[256,768]{1,0:T(8,128)(2,1)S(1)}, u32[]{:S(2)}, u32[]{:S(2)}) collective-permute-start(bf16[256,768]{1,0:T(8,128)(2,1)S(1)} %get-tuple-element.16), channel_id=1, source_target_pairs={{0,64},{64,0},{1,65},{65,1},{2,66},{66,2},{3,67},{67,3},{4,68},{68... | collective-permute-start | bytes 1179656 | tf_op jit(solution)/shard_map/ppermute | solution.py:303
  63.8 0.8 own_term.1.keep_ref
  64.5 0.6 collective-permute-done.got_ref
  65.1 0.2 pair_sum.1
  65.3 15.8 %all_to_all.24 = bf16[8,32,768]{2,1,0:T(8,128)(2,1)S(1)} all-to-all(bf16[8,32,768]{2,1,0:T(8,128)(2,1)S(1)} %pair_sum.1), channel_id=1, replica_groups={{0,128,256,384,512,640,768,896},{1,129,257,385,513,641,769,897},{2,130,..., dimensions={0} | all-to-all | bytes 786432 | tf_op jit(solution)/shard_map/all_to_all | solution.py:307
  81.1 0.1 convert_reduce_fusion
  81.1 0.2 copy.12
  81.3 0.2 copy.13
  81.5 0.1 copy.14
  81.7 34.8 %all_to_all.25 = f32[64,1,384]{2,1,0:T(1,128)S(1)} all-to-all(f32[64,1,384]{2,1,0:T(1,128)S(1)} %copy.14), channel_id=1, replica_groups={{0,1,2,3,4,5,6,7,8,9,10,11,12,13,14,15,16,17,18,19,20,21,22,23,24,25,26..., dimensions={0} | all-to-all | bytes 196608 | tf_op jit(solution)/shard_map/all_to_all | solution.py:313
  116.5 0.1 reduce_sum.19
  116.6 0.7 reshape.35
  (1 shorter events, 0.0 us)
Async XLA Ops:
  0.0 14.4 %all-to-all-start = ((s32[16,1,64]{2,1,0:T(1,128)}), s32[16,1,64]{2,1,0:T(1,128)S(1)}, u32[]{:S(2)}, u32[]{:S(2)}) async-start(s32[16,1,64]{2,1,0:T(1,128)} %bitcast.15), calls=%async_computation | async-start | bytes 16384 | tf_op jit(solution)/shard_map/all_to_all | solution.py:293
  16.2 41.8 %copy-start = (bf16[512,1024]{1,0:T(8,128)(2,1)S(1)}, bf16[512,1024]{1,0:T(8,128)(2,1)}, u32[]{:S(2)}) copy-start(bf16[512,1024]{1,0:T(8,128)(2,1)} %get-tuple-element.11.adj_ref) | copy-start | bytes 3145732
  16.2 41.8 %copy-start.1 = (bf16[768,512]{1,0:T(8,128)(2,1)S(1)}, bf16[768,512]{1,0:T(8,128)(2,1)}, u32[]{:S(2)}) copy-start(bf16[768,512]{1,0:T(8,128)(2,1)} %neigh_ref.1) | copy-start | bytes 2359300
  16.2 41.8 %all-to-all-start.1 = ((bf16[16,64,768]{2,1,0:T(8,128)(2,1)}), bf16[16,64,768]{2,1,0:T(8,128)(2,1)S(1)}, u32[]{:S(2)}, u32[]{:S(2)}) async-start(bf16[16,64,768]{2,1,0:T(8,128)(2,1)} %bitcast.13), calls=%async_computation.1 | async-start | bytes 3145728 | tf_op jit(solution)/shard_map/all_to_all | solution.py:298
  60.9 4.2 %collective-permute-start = (bf16[256,768]{1,0:T(8,128)(2,1)S(1)}, bf16[256,768]{1,0:T(8,128)(2,1)S(1)}, u32[]{:S(2)}, u32[]{:S(2)}) collective-permute-start(bf16[256,768]{1,0:T(8,128)(2,1)S(1)} %get-tuple-element.16), channel_id=1, source_target_pairs={{0,64},{64,0},{1,65},{65,1},{2,66},{66,2},{3,67},{67,3},{4,68},{68... | collective-permute-start | bytes 1179656 | tf_op jit(solution)/shard_map/ppermute | solution.py:303
